TPU v7x, 256 devices: a whole 4x4x8 slice. The times are simulated.
256 devices in a mesh: row: 16 (over y_lo, x, core), col: 16 (over z, y_hi).
Axes of the slice: x: 4, y: 4 (y_hi: 2, y_lo: 2; y = y_hi * 2 + y_lo), z: 8, core: 2. Of those that a mesh axis runs over, the one named last changes fastest.
Arguments:
- pair_act: float32 [768, 768, 128], P('row', 'col'), may hold values from -6 to 6
- residue_mask: int32 [768], replicated, may hold values 0 or 1
- norm_in_gain: float32 [128], replicated, may hold values from 0.1 to 1.9
- norm_in_bias: float32 [128], replicated, may hold values from -3 to 3
- proj_in: bfloat16 [128, 640], replicated, may hold values from -0.5 to 0.5
- proj_bias: float32 [640], replicated, may hold values from -3 to 3
- norm_out_gain: float32 [128], replicated, may hold values from 0.1 to 1.9
- norm_out_bias: float32 [128], replicated, may hold values from -3 to 3
- proj_out: bfloat16 [128, 128], replicated, may hold values from -0.5 to 0.5
- out_bias: float32 [128], replicated, may hold values from -3 to 3
Outputs:
- update: float32 [768, 768, 128], P('row', 'col')
All inputs are finite; a program needn't handle non-finite values.
Results may differ from a plain program's by a relative error of at most 0.0028.
Values may be sent and summed in bfloat16 or wider, within the bound.
No kernel may reach another device: no remote copies, remote signals or barrier semaphores. Data moves between devices by JAX's collectives and lax.ppermute only.
A program may use at most 128 MiB of HBM per device.

v0:
```python
import jax
import jax.numpy as jnp
from jax import lax
from jax.sharding import PartitionSpec as P

CH = 128


def layer_norm(values, gain_vec, bias_vec):
    center = jnp.mean(values, axis=-1, keepdims=True)
    spread = jnp.mean(jnp.square(values - center), axis=-1, keepdims=True)
    return (values - center) * lax.rsqrt(spread + 1e-05) * gain_vec + bias_vec


def body(
    pair_act,
    residue_mask,
    norm_in_gain,
    norm_in_bias,
    proj_in,
    proj_bias,
    norm_out_gain,
    norm_out_bias,
    proj_out,
    out_bias,
):
    tile_rows = pair_act.shape[0]
    tile_cols = pair_act.shape[1]
    normed = layer_norm(pair_act, norm_in_gain, norm_in_bias).astype(jnp.bfloat16)
    projected = jnp.dot(normed, proj_in, preferred_element_type=jnp.float32) + proj_bias
    mask_float = residue_mask.astype(jnp.float32)
    row_mask = lax.dynamic_slice_in_dim(mask_float, lax.axis_index("row") * tile_rows, tile_rows)
    col_mask = lax.dynamic_slice_in_dim(mask_float, lax.axis_index("col") * tile_cols, tile_cols)
    pair_mask = (row_mask[:, None] * col_mask[None, :])[:, :, None]
    left_side = (
        pair_mask * jax.nn.sigmoid(projected[:, :, :CH]) * projected[:, :, CH : 2 * CH]
    ).astype(jnp.bfloat16)
    right_side = (
        pair_mask
        * jax.nn.sigmoid(projected[:, :, 2 * CH : 3 * CH])
        * projected[:, :, 3 * CH : 4 * CH]
    ).astype(jnp.bfloat16)
    out_gate = jax.nn.sigmoid(projected[:, :, 4 * CH :])
    left_all = lax.all_gather(left_side, "col", axis=1, tiled=True)
    left_panel = lax.all_to_all(left_all, "row", split_axis=1, concat_axis=0, tiled=True)
    triangle = jnp.einsum(
        "kic,kjc->ijc",
        left_panel,
        lax.all_gather(right_side, "row", axis=0, tiled=True),
        preferred_element_type=jnp.float32,
    )
    mixed = layer_norm(triangle, norm_out_gain, norm_out_bias).astype(jnp.bfloat16)
    output_lin = jnp.dot(mixed, proj_out, preferred_element_type=jnp.float32) + out_bias
    return out_gate * output_lin


def solution(mesh):
    return jax.shard_map(
        body,
        mesh=mesh,
        in_specs=(P("row", "col", None), P(), P(), P(), P(), P(), P(), P(), P(), P()),
        out_specs=P("row", "col", None),
        check_vma=False,
    )
```

profile of v0, /device:TPU:1, one launch (start us, length us, event | category | flops | bytes accessed | tf_op | source)
XLA Modules:
  0.0 385.3 jit_solution(11096743094885092464)
XLA Ops:
  6.5 0.8 convert_element_type.16
  7.3 1.7 reduce_sum.36
  9.1 0.7 multiply_reduce_fusion.1
  9.8 0.1 fusion.20
  9.9 0.1 broadcast_multiply_fusion
  10.0 1.1 broadcast_add_fusion
  11.1 2.2 fusion.1
  13.3 0.7 copy-done.2
  14.1 0.7 all-gather.3.cloned.1.call-update
  14.8 149.2 %all-gather.5.cloned.1.call-done = bf16[48,768,128]{2,1,0:T(8,128)(2,1)} async-done(((bf16[48,48,128]{2,1,0:T(8,128)(2,1)}), bf16[48,768,128]{2,1,0:T(8,128)(2,1)}) %all-gather.5.cloned.1.call-update) | async-done | bytes 9437200 | tf_op jit(solution)/shard_map/all_gather | solution.py:44
  163.9 13.4 %copy.36 = bf16[48,768,128]{2,0,1:T(8,128)(2,1)} copy(bf16[48,768,128]{2,1,0:T(8,128)(2,1)} %all-gather.5.cloned.1.call-done) | data formatting | bytes 18874368 | tf_op jit(solution)/shard_map/all_gather | solution.py:44
  177.3 5.6 %all-to-all-start = ((bf16[48,768,128]{2,0,1:T(8,128)(2,1)}), bf16[48,768,128]{2,0,1:T(8,128)(2,1)}, u32[]{:S(2)}, u32[]{:S(2)}) async-start(bf16[48,768,128]{2,0,1:T(8,128)(2,1)} %copy.36), calls=%async_computation | async-start | bytes 18874368 | tf_op jit(solution)/shard_map/all_to_all | solution.py:45
  183.0 141.2 %all-gather.3.cloned.1.call-done = bf16[768,48,128]{2,1,0:T(8,128)(2,1)} async-done(((bf16[48,48,128]{2,1,0:T(8,128)(2,1)}), bf16[768,48,128]{2,1,0:T(8,128)(2,1)}) %all-gather.3.cloned.1.call-update) | async-done | bytes 9437200 | tf_op jit(solution)/shard_map/all_gather | solution.py:49
  324.1 14.0 %copy.39 = bf16[768,48,128]{0,1,2:T(8,128)(2,1)} copy(bf16[768,48,128]{2,1,0:T(8,128)(2,1)} %all-gather.3.cloned.1.call-done) | data formatting | bytes 18874368 | tf_op jit(solution)/shard_map/all_gather | solution.py:49
  338.1 9.7 %copy.38 = bf16[16,48,48,128]{3,2,1,0:T(8,128)(2,1)} copy(bf16[16,48,48,128]{3,1,2,0:T(8,128)(2,1)} %bitcast.3) | data formatting | bytes 18874368 | tf_op jit(solution)/shard_map/all_to_all | solution.py:45
  347.8 14.0 %copy.40 = bf16[768,48,128]{0,1,2:T(8,128)(2,1)} copy(bf16[768,48,128]{2,1,0:T(8,128)(2,1)} %bitcast.20) | data formatting | bytes 18874368 | tf_op jit(solution)/shard_map/all_to_all | solution.py:45
  361.8 9.0 %bitcast_reduce_fusion = (f32[48,48]{0,1:T(8,128)S(1)}, f32[128,48,48]{2,1,0:T(8,128)S(1)}) fusion(bf16[768,48,128]{0,1,2:T(8,128)(2,1)} %copy.39, bf16[768,48,128]{0,1,2:T(8,128)(2,1)} %copy.40), kind=kOutput, calls=%fused_computation.1 | convolution fusion | flops 453277440 | bytes 20063232 | tf_op jit(solution)/shard_map/kic,kjc->ijc/dot_general | solution.py:46
  370.8 0.1 copy.41
  371.0 0.5 multiply_reduce_fusion
  371.4 0.1 copy.43
  371.5 0.1 copy.44
  371.6 1.7 add_convert_fusion
  373.4 2.3 copy.45
  375.7 2.7 fusion
  (30 shorter events, 0.2 us)
Async XLA Ops:
  6.5 3.4 copy-start
  6.5 2.5 copy-start.3
  6.5 157.4 %all-gather.5.cloned.1.call-start = ((), (), s32[]{:S(2)}) async-start(), calls=%async_computation.2 | async-start | bytes 10027008 | tf_op jit(solution)/shard_map/all_gather | solution.py:44
  7.3 2.6 copy-start.4
  7.3 2.6 copy-start.5
  7.3 2.6 copy-start.6
  11.1 2.9 copy-start.2
  14.0 310.1 %all-gather.3.cloned.1.call-start = ((), (), s32[]{:S(2)}) async-start(), calls=%async_computation.1 | async-start | bytes 10027008 | tf_op jit(solution)/shard_map/all_gather | solution.py:49
  177.3 160.8 %all-to-all-start = ((bf16[48,768,128]{2,0,1:T(8,128)(2,1)}), bf16[48,768,128]{2,0,1:T(8,128)(2,1)}, u32[]{:S(2)}, u32[]{:S(2)}) async-start(bf16[48,768,128]{2,0,1:T(8,128)(2,1)} %copy.36), calls=%async_computation | async-start | bytes 18874368 | tf_op jit(solution)/shard_map/all_to_all | solution.py:45
  371.0 0.7 copy-start.7
  371.0 0.7 copy-start.8
  373.4 2.3 copy-start.9
  373.4 2.3 copy-start.10
  375.7 2.8 copy-start.1
Sparse Core Ops, SparseCore 0:
  14.1 149.7 all-gather.4
  165.8 158.2 all-gather.2
where the time goes:
time: 390 us; the launch traced here: 385 us
  waiting for transfers between devices  291 us (75%)
  local copies, waits for them, and re-layouts  54.5 us (14%)
  between operations  13.5 us (3%)
  matrix products  12.8 us (3%)
  other arithmetic  7.69 us (2%)
  starting transfers between devices  5.68 us (1%)
    all_gather x1, waiting for transfers between devices, body(): left_all = lax.all_gather(left_side, 'col', axis=1, tiled=True)  149 us
    all_gather x1, waiting for transfers between devices, body(): lax.all_gather(right_side, 'row', axis=0, tiled=True)  141 us
    all_to_all x2, local copies, waits for them, and re-layouts, body(): lax.all_to_all(left_all, 'row', split_axis=1, concat_axis=0, tiled=True)  23.7 us
    all_gather x1, local copies, waits for them, and re-layouts, body(): lax.all_gather(right_side, 'row', axis=0, tiled=True)  14 us
    all_gather x1, local copies, waits for them, and re-layouts, body(): left_all = lax.all_gather(left_side, 'col', axis=1, tiled=True)  13.4 us
    dot_general x1, matrix products, body(): jnp.einsum('kic,kjc->ijc', left_panel, lax.all_gather(right_side, 'row',...  8.97 us
  transfers between devices with their start and end apart: 3, of which 2 were waited for; matrix products, arithmetic and copies ran while one was open for 7% of the time, Pallas kernels for 0%

commit v1 on v0

v1 whole, which is shorter than its diff:
```python
import jax
import jax.numpy as jnp
from jax import lax
from jax.sharding import Mesh
from jax.sharding import PartitionSpec as P

CH = 128
ROW = ("y_lo", "x", "core")
COL = ("z", "y_hi")
CHIPS = ("y_lo", "x", "z", "y_hi")
SWAP = [(0, 1), (1, 0)]


def layer_norm(values, gain_vec, bias_vec, axis):
    center = jnp.mean(values, axis=axis, keepdims=True)
    spread = jnp.mean(jnp.square(values - center), axis=axis, keepdims=True)
    return (values - center) * lax.rsqrt(spread + 1e-05) * gain_vec + bias_vec


def body(
    pair_act,
    residue_mask,
    norm_in_gain,
    norm_in_bias,
    proj_in,
    proj_bias,
    norm_out_gain,
    norm_out_bias,
    proj_out,
    out_bias,
):
    rows, cols, chans = pair_act.shape
    block = rows * cols
    n_pair, n_col = lax.axis_size(("y_lo", "x")), lax.axis_size(COL)
    core = lax.axis_index("core")
    flat = pair_act.reshape(block, chans)
    normed = layer_norm(flat, norm_in_gain, norm_in_bias, -1).astype(jnp.bfloat16)
    sides = lax.dot_general(
        proj_in[:, : 4 * CH], normed, (((0,), (1,)), ((), ())), preferred_element_type=jnp.float32
    ) + proj_bias[: 4 * CH, None]
    mask_float = residue_mask.astype(jnp.float32)
    row_mask = lax.dynamic_slice_in_dim(mask_float, lax.axis_index(ROW) * rows, rows)
    col_mask = lax.dynamic_slice_in_dim(mask_float, lax.axis_index(COL) * cols, cols)
    pair_mask = (row_mask[:, None] * col_mask[None, :]).reshape(1, block)
    left = (pair_mask * jax.nn.sigmoid(sides[:CH]) * sides[CH : 2 * CH]).astype(jnp.bfloat16)
    right = (
        pair_mask * jax.nn.sigmoid(sides[2 * CH : 3 * CH]) * sides[3 * CH :]
    ).astype(jnp.bfloat16)
    packed = jnp.stack([left, right], axis=1)
    packed = lax.all_to_all(packed, CHIPS, 0, 0, tiled=True)
    packed = packed.reshape(n_pair, n_col // 2, 2, 2, rows, cols)
    left_m = packed[:, :, :, 0].transpose(0, 3, 2, 1, 4).reshape(n_pair * rows, 2, n_col // 2 * cols)
    right_m = packed[:, :, :, 1].transpose(0, 3, 1, 2, 4).reshape(n_pair * rows, n_col * cols)
    left_mine = lax.dynamic_index_in_dim(left_m, core, 1, keepdims=False)
    left_send = lax.dynamic_index_in_dim(left_m, 1 - core, 1, keepdims=False)
    left_got = lax.ppermute(left_send, "core", SWAP)
    right_got = lax.ppermute(right_m, "core", SWAP)
    dims = (((0,), (0,)), ((), ()))
    triangle = lax.dot_general(left_mine, right_m, dims, preferred_element_type=jnp.float32)
    triangle += lax.dot_general(left_got, right_got, dims, preferred_element_type=jnp.float32)
    triangle = triangle.astype(jnp.bfloat16)
    triangle = triangle.reshape(n_pair, rows, n_col, cols).transpose(0, 2, 1, 3)
    triangle = lax.all_to_all(triangle.reshape(-1, 18, 128), CHIPS, 0, 0, tiled=True)
    triangle = triangle.reshape(CH, block).astype(jnp.float32)
    mixed = layer_norm(triangle, norm_out_gain[:, None], norm_out_bias[:, None], 0)
    high = mixed.astype(jnp.bfloat16)
    low = (mixed - high.astype(jnp.float32)).astype(jnp.bfloat16)
    output_lin = (
        lax.dot_general(high, proj_out, dims, preferred_element_type=jnp.float32)
        + lax.dot_general(low, proj_out, dims, preferred_element_type=jnp.float32)
        + out_bias
    )
    out_gate = jax.nn.sigmoid(
        jnp.dot(normed, proj_in[:, 4 * CH :], preferred_element_type=jnp.float32)
        + proj_bias[4 * CH :]
    )
    return (out_gate * output_lin).reshape(rows, cols, chans)


def solution(mesh):
    fine = Mesh(mesh.devices.reshape(2, 4, 2, 8, 2), ROW + COL)
    return jax.shard_map(
        body,
        mesh=fine,
        in_specs=(P(ROW, COL, None), P(), P(), P(), P(), P(), P(), P(), P(), P()),
        out_specs=P(ROW, COL, None),
        check_vma=False,
    )
```

time: 390 us -> 117 us (0.30); the launches traced: 385 us -> 116 us
  waiting for transfers between devices: 291 us -> 22.5 us
  blocking collectives: 0 us -> 45.9 us
  local copies, waits for them, and re-layouts: 54.5 us -> 23.8 us
  between operations: 13.5 us -> 0.33 us
  matrix products: 12.8 us -> 4.91 us
  starting transfers between devices: 5.68 us -> 11.9 us
    all_gather x2 -> x0, waiting for transfers between devices: 290 us -> none  [the longest x1 149 us: body(): left_all = lax.all_gather(left_side, 'col', axis=1, tiled=True)]
    all_to_all x0 -> x1, blocking collectives: none -> 45.9 us  [body(): packed = lax.all_to_all(packed, CHIPS, 0, 0, tiled=True)]
    all_gather x2 -> x0, local copies, waits for them, and re-layouts: 27.4 us -> none  [the longest x1 14 us: body(): lax.all_gather(right_side, 'row', axis=0, tiled=True)]
    all_to_all x2 -> x1, local copies, waits for them, and re-layouts: 23.7 us -> 1.13 us  [body(): packed = lax.all_to_all(packed, CHIPS, 0, 0, tiled=True)]
    all_to_all x1, waiting for transfers between devices: 0.01 us -> 21.5 us  [body(): lax.all_to_all(triangle.reshape(-1, 18, 128), CHIPS, 0, 0, tiled=True)]
    reshape x0 -> x6, local copies, waits for them, and re-layouts: none -> 13.9 us  [the longest x1 5.28 us: body(): packed = packed.reshape(n_pair, n_col // 2, 2, 2, rows, cols)]
    dot_general x3 -> x6, matrix products: 12.8 us -> 4.91 us  [the longest x1 1.57 us: body(): lax.dot_general(left_got, right_got, dims, preferred_element_type=jnp.flo...]
    transpose x0 -> x3, local copies, waits for them, and re-layouts: none -> 4.92 us  [the longest x2 2.88 us: body(): packed[:, :, :, 0].transpose(0, 3, 2, 1, 4)]
  transfers between devices with their start and end apart: 3 -> 3, of which waited for: 2 -> 2; matrix products, arithmetic and copies ran while one was open for 7% -> 2% of each run, Pallas kernels for 0% -> 0%
where the time goes in v1:
time: 117 us; the launch traced here: 116 us
  blocking collectives  45.9 us (39%)
  local copies, waits for them, and re-layouts  23.8 us (20%)
  waiting for transfers between devices  22.5 us (19%)
  starting transfers between devices  11.9 us (10%)
  other arithmetic  6.9 us (6%)
  matrix products  4.91 us (4%)
    all_to_all x1, blocking collectives, body(): packed = lax.all_to_all(packed, CHIPS, 0, 0, tiled=True)  45.9 us
    all_to_all x1, waiting for transfers between devices, body(): lax.all_to_all(triangle.reshape(-1, 18, 128), CHIPS, 0, 0, tiled=True)  21.5 us
    all_to_all x1, starting transfers between devices, body(): lax.all_to_all(triangle.reshape(-1, 18, 128), CHIPS, 0, 0, tiled=True)  8.86 us
    reshape x1, local copies, waits for them, and re-layouts, body(): packed = packed.reshape(n_pair, n_col // 2, 2, 2, rows, cols)  5.28 us
    reshape x1, local copies, waits for them, and re-layouts, body(): triangle.reshape(-1, 18, 128)  3.36 us
    transpose x2, local copies, waits for them, and re-layouts, body(): packed[:, :, :, 0].transpose(0, 3, 2, 1, 4)  2.88 us
    ppermute x1, starting transfers between devices, body(): right_got = lax.ppermute(right_m, 'core', SWAP)  2.73 us
    reshape x2, local copies, waits for them, and re-layouts, body(): triangle = triangle.reshape(n_pair, rows, n_col, cols).transpose(0, 2, 1, 3)  2.35 us
  transfers between devices with their start and end apart: 3, of which 2 were waited for; matrix products, arithmetic and copies ran while one was open for 2% of the time, Pallas kernels for 0%

profile of v1, /device:TPU:1, one launch (start us, length us, event | category | flops | bytes accessed | tf_op | source)
XLA Modules:
  0.0 116.3 jit_solution(18144561334350448576)
XLA Ops:
  0.0 1.7 %reduce_sum.36 = f32[48,48]{1,0:T(8,128)S(1)} reduce(f32[48,48,128]{2,1,0:T(8,128)} %param.10, f32[]{:T(128)} %constant.19.clone.1), dimensions={2}, to_apply=%region_0.0 | reduce | flops 292608 | bytes 1188868 | tf_op jit(solution)/shard_map/reduce_sum | solution.py:15
  1.8 0.7 multiply_reduce_fusion.1
  3.0 1.3 %fusion.24 = bf16[2304,128]{1,0:T(8,128)(2,1)S(1)} fusion(f32[48,48,128]{2,1,0:T(8,128)S(1)} %copy-done.1, f32[128]{0:T(128)S(1)} %copy-done.9, f32[128]{0:T(128)S(1)} %copy-done.10, f32[2304]{0:T(1024)S(1)} %rsqrt.23, f32[2304]{0:T(1024)S(1)} %div.26), kind=kLoop, calls=%fused_computation.39 | loop fusion | flops 1474560 | bytes 1788928 | tf_op jit(solution)/shard_map/convert_element_type | solution.py:37
  4.3 0.8 copy-done.3
  5.1 0.8 fusion
  5.9 1.2 %fusion.26 = (bf16[128,1,2304]{0,2,1:T(8,128)(2,1)S(1)}, bf16[128,1,2304]{0,2,1:T(8,128)(2,1)S(1)}) fusion(f32[512,2304]{0,1:T(8,128)S(1)} %fusion, f32[2304]{0:T(1024)S(1)} %mul.102), kind=kLoop, calls=%fused_computation.44 | loop fusion | flops 3538944 | bytes 5907456 | tf_op jit(solution)/shard_map/stack | solution.py:49
  7.2 1.6 %copy.16 = bf16[128,2,2304]{2,1,0:T(2,128)(2,1)S(1)} copy(bf16[128,2,2304]{0,2,1:T(8,128)(2,1)S(1)} %pad_maximum_fusion) | data formatting | bytes 2359296 | tf_op jit(solution)/shard_map/stack | solution.py:49
  8.8 45.9 %all_to_all.10 = bf16[128,2,2304]{2,1,0:T(2,128)(2,1)S(1)} all-to-all(bf16[128,2,2304]{2,1,0:T(2,128)(2,1)S(1)} %copy.16), channel_id=1, replica_groups=mesh['y_lo'=2,'x'=4,'core'=2,'z'=8,'y_hi'=2] {'y_lo','x','z','y_hi'}, dimensions={0} | all-to-all | bytes 2359296 | tf_op jit(solution)/shard_map/all_to_all | solution.py:50
  54.7 1.1 copy.17
  55.9 5.3 %reshape.113 = bf16[8,8,2,2,48,48]{5,4,2,1,0,3:T(8,128)(2,1)S(1)} reshape(bf16[128,2,2304]{2,0,1:T(8,128)(2,1)} %copy.17) | data formatting | bytes 2359296 | tf_op jit(solution)/shard_map/reshape | solution.py:51
  61.2 2.3 %slice_bitcast_fusion.1 = (bf16[8,48,2,8,48]{4,1,2,3,0:T(8,128)(2,1)}, bf16[8,48,8,2,48]{4,1,3,2,0:T(8,128)(2,1)}) fusion(bf16[8,8,2,2,48,48]{5,4,2,1,0,3:T(8,128)(2,1)S(1)} %reshape.113), kind=kLoop, calls=%fused_computation.11 | loop fusion | bytes 2359296 | tf_op jit(solution)/shard_map/transpose | solution.py:52
  63.4 2.0 %copy.19 = bf16[8,48,8,2,48]{1,0,4,3,2:T(8,128)(2,1)S(1)} copy(bf16[8,48,8,2,48]{4,1,3,2,0:T(8,128)(2,1)} %get-tuple-element.8) | data formatting | bytes 1179648 | tf_op jit(solution)/shard_map/transpose | solution.py:53
  65.5 1.8 %reshape.115 = bf16[384,768]{0,1:T(8,128)(2,1)} reshape(bf16[8,48,8,2,48]{1,0,4,3,2:T(8,128)(2,1)S(1)} %copy.19) | data formatting | bytes 1179648 | tf_op jit(solution)/shard_map/reshape | solution.py:53
  67.3 2.7 %collective-permute-start.1 = (bf16[384,768]{0,1:T(8,128)(2,1)}, bf16[384,768]{0,1:T(8,128)(2,1)}, u32[]{:S(2)}, u32[]{:S(2)}) collective-permute-start(bf16[384,768]{0,1:T(8,128)(2,1)} %reshape.115), channel_id=1, source_target_pairs={{0,16},{16,0},{1,17},{17,1},{2,18},{18,2},{3,19},{19,3},{4,20},{20... | collective-permute-start | bytes 1769480 | tf_op jit(solution)/shard_map/ppermute | solution.py:57
  70.0 0.6 copy.18
  70.7 1.1 reshape.114
  72.6 1.0 collective-permute-done
  73.7 1.6 %fusion.7 = bf16[384,768]{1,0:T(8,128)(2,1)S(1)} fusion(f32[384,768]{1,0:T(8,128)S(1)} %fusion.28, bf16[384,384]{1,0:T(8,128)(2,1)S(1)} %collective-permute-done, bf16[384,768]{0,1:T(8,128)(2,1)} %collective-permute-done.1), kind=kOutput, calls=%fused_computation.15 | convolution fusion | flops 227082240 | bytes 2654208 | tf_op jit(solution)/shard_map/dot_general | solution.py:60
  75.3 1.9 %reshape.116 = bf16[8,48,16,48]{3,2,1,0:T(8,128)(2,1)S(1)} reshape(bf16[384,768]{1,0:T(8,128)(2,1)S(1)} %fusion.7) | data formatting | bytes 1179648 | tf_op jit(solution)/shard_map/reshape | solution.py:62
  77.6 3.4 %reshape.117 = bf16[128,18,128]{2,1,0:T(8,128)(2,1)} reshape(bf16[8,16,48,48]{3,2,1,0:T(8,128)(2,1)S(1)} %bitcast.72) | data formatting | bytes 1179648 | tf_op jit(solution)/shard_map/reshape | solution.py:63
  81.0 8.9 %all-to-all-start.1 = ((bf16[128,18,128]{2,1,0:T(8,128)(2,1)}), bf16[128,18,128]{2,1,0:T(8,128)(2,1)S(1)}, u32[]{:S(2)}, u32[]{:S(2)}) async-start(bf16[128,18,128]{2,1,0:T(8,128)(2,1)} %reshape.117), calls=%async_computation.1 | async-start | bytes 1572864 | tf_op jit(solution)/shard_map/all_to_all | solution.py:63
  90.4 21.5 %all-to-all-done.1 = bf16[128,18,128]{2,1,0:T(8,128)(2,1)S(1)} async-done(((bf16[128,18,128]{2,1,0:T(8,128)(2,1)}), bf16[128,18,128]{2,1,0:T(8,128)(2,1)S(1)}, u32[]{:S(2)}, u32[]{:S(2)}) %all-to-all-start.1) | async-done | bytes 589856 | tf_op jit(solution)/shard_map/all_to_all | solution.py:63
  113.0 1.3 %subtract_convert_fusion = (bf16[128,2304]{0,1:T(8,128)(2,1)S(1)}, bf16[128,2304]{0,1:T(8,128)(2,1)S(1)}) fusion(f32[128,18,128]{0,2,1:T(8,128)S(1)} %copy.21, f32[128]{0:T(128)S(1)} %copy-done.11, f32[128]{0:T(128)S(1)} %copy-done.12, f32[2304]{0:T(1024)S(1)} %rsqrt_bitcast_fusion, f32[2304]{0:T(1024)S(1)} %get-tuple-element.11), kind=kLoop, calls=%fused_computation.40 | loop fusion | flops 2359296 | bytes 2378752 | tf_op jit(solution)/shard_map/convert_element_type | solution.py:67
  114.9 1.3 %fusion.2 = f32[2304,128]{1,0:T(8,128)} fusion(f32[2304,128]{1,0:T(8,128)S(1)} %fusion.6, f32[2304,128]{1,0:T(8,128)S(1)} %fusion.36, bf16[128,2304]{0,1:T(8,128)(2,1)S(1)} %get-tuple-element.9, bf16[128,128]{1,0:T(8,128)(2,1)S(1)} %copy-done, f32[128]{0:T(128)S(1)} %copy-done.13), kind=kOutput, calls=%fused_computation.4 | convolution fusion | flops 76382208 | bytes 4162048 | tf_op jit(solution)/shard_map/dot_general | solution.py:70
  (51 shorter events, 4.0 us)
Async XLA Ops:
  0.0 114.3 %copy-start = (bf16[128,128]{1,0:T(8,128)(2,1)S(1)}, bf16[128,128]{1,0:T(8,128)(2,1)}, u32[]{:S(2)}) copy-start(bf16[128,128]{1,0:T(8,128)(2,1)} %param.18) | copy-start | bytes 98308
  0.0 1.8 %copy-start.1 = (f32[48,48,128]{2,1,0:T(8,128)S(1)}, f32[48,48,128]{2,1,0:T(8,128)}, u32[]{:S(2)}) copy-start(f32[48,48,128]{2,1,0:T(8,128)} %param.10) | copy-start | bytes 3538948
  0.0 2.6 %copy-start.8 = (s32[768]{0:T(1024)S(1)}, s32[768]{0:T(1024)}, u32[]{:S(2)}) copy-start(s32[768]{0:T(1024)} %param.11) | copy-start | bytes 9220
  0.0 2.9 %copy-start.9 = (f32[128]{0:T(128)S(1)}, f32[128]{0:T(128)}, u32[]{:S(2)}) copy-start(f32[128]{0:T(128)} %param.13) | copy-start | bytes 1540
  0.0 2.9 %copy-start.10 = (f32[128]{0:T(128)S(1)}, f32[128]{0:T(128)}, u32[]{:S(2)}) copy-start(f32[128]{0:T(128)} %param.12) | copy-start | bytes 1540
  2.5 2.6 %copy-start.6 = (bf16[128,640]{1,0:T(8,128)(2,1)S(1)}, bf16[128,640]{1,0:T(8,128)(2,1)}, u32[]{:S(2)}) copy-start(bf16[128,640]{1,0:T(8,128)(2,1)} %param.14) | copy-start | bytes 491524
  2.5 2.6 %slice-start = ((f32[640]{0:T(1024)}), f32[512]{0:T(512)S(1)}, s32[]{:S(2)}) async-start(f32[640]{0:T(1024)} %param.15), calls=%async_computation.2 | async-start | bytes 4096 | tf_op jit(solution)/shard_map/slice | solution.py:40
  4.3 0.8 copy-start.3
  65.5 4.6 %copy-start.2 = (bf16[8,48,2,8,48]{4,1,2,3,0:T(8,128)(2,1)S(1)}, bf16[8,48,2,8,48]{4,1,2,3,0:T(8,128)(2,1)}, u32[]{:S(2)}) copy-start(bf16[8,48,2,8,48]{4,1,2,3,0:T(8,128)(2,1)} %get-tuple-element.7) | copy-start | bytes 1769476
  67.3 6.4 %collective-permute-start.1 = (bf16[384,768]{0,1:T(8,128)(2,1)}, bf16[384,768]{0,1:T(8,128)(2,1)}, u32[]{:S(2)}, u32[]{:S(2)}) collective-permute-start(bf16[384,768]{0,1:T(8,128)(2,1)} %reshape.115), channel_id=1, source_target_pairs={{0,16},{16,0},{1,17},{17,1},{2,18},{18,2},{3,19},{19,3},{4,20},{20... | collective-permute-start | bytes 1769480 | tf_op jit(solution)/shard_map/ppermute | solution.py:57
  70.7 1.5 %copy-start.5 = (bf16[384,768]{0,1:T(8,128)(2,1)S(1)}, bf16[384,768]{0,1:T(8,128)(2,1)}, u32[]{:S(2)}) copy-start(bf16[384,768]{0,1:T(8,128)(2,1)} %reshape.115) | copy-start | bytes 1769476
  71.8 1.9 %collective-permute-start = (bf16[384,384]{1,0:T(8,128)(2,1)S(1)}, bf16[384,384]{1,0:T(8,128)(2,1)S(1)}, u32[]{:S(2)}, u32[]{:S(2)}) collective-permute-start(bf16[384,384]{1,0:T(8,128)(2,1)S(1)} %dynamic-slice_bitcast_fusion), channel_id=1, source_target_pairs={{0,16},{16,0},{1,17},{17,1},{2,18},{18,2},{3,19},{19,3},{4,20},{20... | collective-permute-start | bytes 884744 | tf_op jit(solution)/shard_map/ppermute | solution.py:56
  81.0 8.9 %copy-start.7 = (f32[640]{0:T(1024)S(1)}, f32[640]{0:T(1024)}, u32[]{:S(2)}) copy-start(f32[640]{0:T(1024)} %param.15) | copy-start | bytes 7684
  81.0 8.9 %copy-start.4 = (bf16[2304,128]{1,0:T(8,128)(2,1)S(1)}, bf16[2304,128]{1,0:T(8,128)(2,1)}, u32[]{:S(2)}) copy-start(bf16[2304,128]{1,0:T(8,128)(2,1)} %copy-done.3) | copy-start | bytes 1769476
  81.0 30.9 %all-to-all-start.1 = ((bf16[128,18,128]{2,1,0:T(8,128)(2,1)}), bf16[128,18,128]{2,1,0:T(8,128)(2,1)S(1)}, u32[]{:S(2)}, u32[]{:S(2)}) async-start(bf16[128,18,128]{2,1,0:T(8,128)(2,1)} %reshape.117), calls=%async_computation.1 | async-start | bytes 1572864 | tf_op jit(solution)/shard_map/all_to_all | solution.py:63
  112.3 0.7 copy-start.11
  112.3 0.7 copy-start.12
  114.3 0.7 copy-start.13

commit v2 on v0

v2 whole, which is shorter than its diff:
```python
import jax
import jax.numpy as jnp
from jax import lax
from jax.experimental import pallas as pl
from jax.experimental.pallas import tpu as pltpu
from jax.sharding import Mesh
from jax.sharding import PartitionSpec as P

CH = 128
ROW = ("y_lo", "x", "core")
COL = ("z", "y_hi")
CHIPS = ("y_hi", "z", "y_lo", "x")
SWAP = [(0, 1), (1, 0)]
LANES = 128
SIDE = 48
WIDE = 32
THIN = 16
BLOCK = SIDE * SIDE
THIN_AT = SIDE * WIDE
STEP = 8
F32 = jnp.float32
BF16 = jnp.bfloat16
EPS = 1e-05


def regroup(parts, width):
    lane = lax.broadcasted_iota(jnp.int32, parts[0].shape, 1)
    count = LANES // width
    parts = list(parts)
    hop = count // 2
    while hop:
        shift = hop * width
        low = (lane // shift) % 2 == 0
        nxt = list(parts)
        for g in range(count):
            if g & hop == 0:
                a, b = parts[g], parts[g | hop]
                nxt[g] = jnp.where(low, a, pltpu.roll(b, shift, 1))
                nxt[g | hop] = jnp.where(low, pltpu.roll(a, LANES - shift, 1), b)
        parts = nxt
        hop //= 2
    return parts


def rows_of(act_ref, at):
    block = act_ref[at : at + STEP]
    return jnp.concatenate(
        [
            block[:, :WIDE].reshape(STEP * WIDE, LANES),
            block[:, WIDE:].reshape(STEP * THIN, LANES),
        ],
        axis=0,
    )


def norm_rows(values, gain, bias):
    center = jnp.mean(values, axis=-1, keepdims=True)
    off = values - center
    spread = jnp.mean(jnp.square(off), axis=-1, keepdims=True)
    return (off * lax.rsqrt(spread + EPS) * gain + bias).astype(BF16)


def sides_kernel(act_ref, row_ref, col_ref, gain_ref, bias_ref, w_ref, wb_ref, out_ref, wt_ref):
    wt_ref[...] = w_ref[:, : 4 * CH].T
    lanes = STEP * SIDE
    place = lax.broadcasted_iota(jnp.int32, (SIDE, lanes), 1)
    index = lax.broadcasted_iota(jnp.int32, (SIDE, lanes), 0)
    wide = place < STEP * WIDE
    k_of = jnp.where(wide, place // WIDE, (place - STEP * WIDE) // THIN)
    i_of = jnp.where(wide, place % WIDE, WIDE + (place - STEP * WIDE) % THIN)
    col_mask = jnp.dot(col_ref[...], (i_of == index).astype(F32), preferred_element_type=F32)
    for at in range(0, SIDE, STEP):
        row_mask = jnp.dot(
            row_ref[...], (k_of + at == index).astype(F32), preferred_element_type=F32
        )
        mask = (row_mask * col_mask)[:1]
        normed = norm_rows(rows_of(act_ref, at), gain_ref[...], bias_ref[...])
        for side in range(2):
            both = (
                lax.dot_general(
                    wt_ref[side * 2 * CH : (side + 1) * 2 * CH],
                    normed,
                    (((1,), (1,)), ((), ())),
                    preferred_element_type=F32,
                )
                + wb_ref[side * 2 * CH : (side + 1) * 2 * CH]
            )
            value = (mask * jax.nn.sigmoid(both[:CH]) * both[CH:]).astype(BF16)
            out_ref[side, :, at * WIDE : (at + STEP) * WIDE] = value[:, : STEP * WIDE]
            out_ref[side, :, THIN_AT + at * THIN : THIN_AT + (at + STEP) * THIN] = value[
                :, STEP * WIDE :
            ]


def gate_kernel(act_ref, gain_ref, bias_ref, w_ref, wb_ref, out_ref):
    for at in range(0, SIDE, STEP):
        normed = norm_rows(rows_of(act_ref, at), gain_ref[...], bias_ref[...])
        lin = jnp.dot(normed, w_ref[...], preferred_element_type=F32) + wb_ref[...]
        out_ref[at * SIDE : (at + STEP) * SIDE] = jax.nn.sigmoid(lin)


def gather_k(mine, got, blocks, dst_ref):
    for width, lanes_at, col_at in ((WIDE, 0, 0), (THIN, THIN_AT, blocks * WIDE)):
        count = LANES // width
        for group in range(blocks // count):
            for piece in range(SIDE // count):
                lanes = slice(lanes_at + piece * LANES, lanes_at + (piece + 1) * LANES)
                halves = []
                for ref in (mine, got):
                    parts = []
                    for pair in range(count // 2):
                        row = (group * count + 2 * pair) * 8
                        two = ref[row : row + 16, lanes].astype(F32)
                        parts += [two[:8], two[8:]]
                    halves.append(regroup(parts, width))
                for b in range(count):
                    k = piece * count + b
                    both = jnp.concatenate([halves[0][b], halves[1][b]], axis=0).astype(BF16)
                    dst_ref[
                        16 * k : 16 * (k + 1), col_at + group * LANES : col_at + (group + 1) * LANES
                    ] = both


def triangle_kernel(lm_ref, lg_ref, rm_ref, rg_ref, out_ref, left_ref, right_ref, tri_ref):
    gather_k(lm_ref, lg_ref, 8, left_ref)
    gather_k(rm_ref, rg_ref, 16, right_ref)
    product = lax.dot_general(
        left_ref[...], right_ref[...], (((0,), (0,)), ((), ())), preferred_element_type=F32
    )
    for strip in range(tri_ref.shape[0]):
        tri_ref[strip] = product[:, strip * LANES : (strip + 1) * LANES]
    for width, lanes_at, col_at in ((WIDE, 0, 0), (THIN, THIN_AT, 16 * WIDE)):
        count = LANES // width
        for group in range(16 // count):
            strip = tri_ref.at[col_at // LANES + group]
            for piece in range(SIDE // count):
                parts = []
                for b in range(count):
                    i = piece * count + b
                    if i < WIDE:
                        parts.append(strip[pl.ds(i, 8, stride=WIDE), :])
                    else:
                        parts.append(strip[pl.ds(8 * WIDE + i - WIDE, 8, stride=THIN), :])
                parts = regroup(parts, width)
                for pair in range(count // 2):
                    row = (group * count + 2 * pair) * 8
                    out_ref[
                        row : row + 16, lanes_at + piece * LANES : lanes_at + (piece + 1) * LANES
                    ] = jnp.concatenate(parts[2 * pair : 2 * pair + 2], axis=0).astype(BF16)


def finish_kernel(tri_ref, gate_ref, gain_ref, bias_ref, w_ref, wb_ref, out_ref):
    twice = jnp.concatenate([w_ref[...], w_ref[...]], axis=0)
    for at in range(0, SIDE, STEP):
        tri = jnp.concatenate(
            [
                tri_ref[:, at * WIDE : (at + STEP) * WIDE],
                tri_ref[:, THIN_AT + at * THIN : THIN_AT + (at + STEP) * THIN],
            ],
            axis=1,
        ).astype(F32)
        off = tri - jnp.mean(tri, axis=0, keepdims=True)
        spread = jnp.mean(jnp.square(off), axis=0, keepdims=True)
        mixed = off * lax.rsqrt(spread + EPS) * gain_ref[...] + bias_ref[...]
        high = mixed.astype(BF16)
        low = (mixed - high.astype(F32)).astype(BF16)
        lin = lax.dot_general(
            jnp.concatenate([high, low], axis=0),
            twice,
            (((0,), (0,)), ((), ())),
            preferred_element_type=F32,
        )
        update = gate_ref[at * SIDE : (at + STEP) * SIDE] * (lin + wb_ref[...])
        out_ref[at : at + STEP, :WIDE] = update[: STEP * WIDE].reshape(STEP, WIDE, LANES)
        out_ref[at : at + STEP, WIDE:] = update[STEP * WIDE :].reshape(STEP, THIN, LANES)


def call(kernel, shape, dtype, scratch=(), flops=10**8):
    return pl.pallas_call(
        kernel,
        out_shape=jax.ShapeDtypeStruct(shape, dtype),
        scratch_shapes=scratch,
        compiler_params=pltpu.CompilerParams(vmem_limit_bytes=40 * 2**20),
        cost_estimate=pl.CostEstimate(flops=flops, bytes_accessed=3 * 10**6, transcendentals=0),
    )


def body(
    pair_act,
    residue_mask,
    norm_in_gain,
    norm_in_bias,
    proj_in,
    proj_bias,
    norm_out_gain,
    norm_out_bias,
    proj_out,
    out_bias,
):
    core = lax.axis_index("core")
    mask_float = residue_mask.astype(F32)
    row_mask = lax.dynamic_slice_in_dim(mask_float, lax.axis_index(ROW) * SIDE, SIDE)
    col_mask = lax.dynamic_slice_in_dim(mask_float, lax.axis_index(COL) * SIDE, SIDE)
    gain_in, bias_in = norm_in_gain[None], norm_in_bias[None]
    sides = call(
        sides_kernel, (2, CH, BLOCK), BF16, [pltpu.VMEM((4 * CH, LANES), BF16)]
    )(
        pair_act,
        jnp.broadcast_to(row_mask[None], (8, SIDE)),
        jnp.broadcast_to(col_mask[None], (8, SIDE)),
        gain_in,
        bias_in,
        proj_in,
        proj_bias[:, None],
    )
    packed = sides.transpose(1, 0, 2)
    packed = lax.all_to_all(packed, CHIPS, 0, 0, tiled=True)
    left, right = packed[:, 0], packed[:, 1]
    half = CH // 2
    left_mine = lax.dynamic_slice_in_dim(left, core * half, half)
    left_send = lax.dynamic_slice_in_dim(left, (1 - core) * half, half)
    left_got = lax.ppermute(left_send, "core", SWAP)
    right_got = lax.ppermute(right, "core", SWAP)
    triangle = call(
        triangle_kernel,
        (CH, BLOCK),
        BF16,
        [
            pltpu.VMEM((16 * SIDE, 8 * SIDE), BF16),
            pltpu.VMEM((16 * SIDE, 16 * SIDE), BF16),
            pltpu.VMEM((6, 8 * SIDE, LANES), F32),
        ],
    )(left_mine, left_got, right, right_got)
    gate = call(gate_kernel, (BLOCK, CH), F32)(
        pair_act, gain_in, bias_in, proj_in[:, 4 * CH :], proj_bias[None, 4 * CH :]
    )
    triangle = triangle.reshape(CH, 2, BLOCK // 2)
    triangle = lax.all_to_all(triangle, CHIPS, 0, 0, tiled=True).reshape(CH, BLOCK)
    return call(finish_kernel, (SIDE, SIDE, CH), F32)(
        triangle, gate, norm_out_gain[:, None], norm_out_bias[:, None], proj_out, out_bias[None]
    )


def solution(mesh):
    fine = Mesh(mesh.devices.reshape(2, 4, 2, 8, 2), ROW + COL)
    return jax.shard_map(
        body,
        mesh=fine,
        in_specs=(P(ROW, COL, None), P(), P(), P(), P(), P(), P(), P(), P(), P()),
        out_specs=P(ROW, COL, None),
        check_vma=False,
    )
```

time: 390 us -> 117 us (0.30); the launches traced: 385 us -> 116 us
  waiting for transfers between devices: 291 us -> 52.9 us
  local copies, waits for them, and re-layouts: 54.5 us -> 12.4 us
  Pallas kernels: 0 us -> 24.3 us
  starting transfers between devices: 5.68 us -> 26.1 us
  between operations: 13.5 us -> 0.17 us
  matrix products: 12.8 us -> 0 us
  other arithmetic: 7.69 us -> 0.69 us
    all_gather x2 -> x0, waiting for transfers between devices: 290 us -> none  [the longest x1 149 us: body(): left_all = lax.all_gather(left_side, 'col', axis=1, tiled=True)]
    all_to_all x1 -> x2, waiting for transfers between devices: 0.01 us -> 51.4 us  [the longest x1 32.4 us: body(): packed = lax.all_to_all(packed, CHIPS, 0, 0, tiled=True)]
    all_gather x2 -> x0, local copies, waits for them, and re-layouts: 27.4 us -> none  [the longest x1 14 us: body(): lax.all_gather(right_side, 'row', axis=0, tiled=True)]
    pallas_call x0 -> x4, Pallas kernels: none -> 24.3 us  [the longest x1 19.7 us: body(): call(triangle_kernel, (CH, BLOCK), BF16, [pltpu.VMEM((16 * SIDE, 8 * SIDE...]
    all_to_all x2 -> x0, local copies, waits for them, and re-layouts: 23.7 us -> none  [body(): lax.all_to_all(left_all, 'row', split_axis=1, concat_axis=0, tiled=True)]
    all_to_all x1 -> x2, starting transfers between devices: 5.63 us -> 22.5 us  [the longest x1 16.3 us: body(): packed = lax.all_to_all(packed, CHIPS, 0, 0, tiled=True)]
    dot_general x3 -> x0, matrix products: 12.8 us -> none  [the longest x1 8.97 us: body(): jnp.einsum('kic,kjc->ijc', left_panel, lax.all_gather(right_side, 'row',...]
    convert_element_type x3 -> x1, other arithmetic: 4.73 us -> 0.69 us  [body(): mask_float = residue_mask.astype(F32)]
  transfers between devices with their start and end apart: 3 -> 4, of which waited for: 2 -> 3; matrix products, arithmetic and copies ran while one was open for 7% -> 3% of each run, Pallas kernels for 0% -> 1%
where the time goes in v2:
time: 117 us; the launch traced here: 116 us
  waiting for transfers between devices  52.9 us (45%)
  starting transfers between devices  26.1 us (22%)
  Pallas kernels  24.3 us (21%)
  local copies, waits for them, and re-layouts  12.4 us (11%)
    all_to_all x1, waiting for transfers between devices, body(): packed = lax.all_to_all(packed, CHIPS, 0, 0, tiled=True)  32.4 us
    pallas_call x1, Pallas kernels, body(): call(triangle_kernel, (CH, BLOCK), BF16, [pltpu.VMEM((16 * SIDE, 8 * SIDE...  19.7 us
    all_to_all x1, waiting for transfers between devices, body(): lax.all_to_all(triangle, CHIPS, 0, 0, tiled=True).reshape(CH, BLOCK)  18.9 us
    all_to_all x1, starting transfers between devices, body(): packed = lax.all_to_all(packed, CHIPS, 0, 0, tiled=True)  16.3 us
    all_to_all x1, starting transfers between devices, body(): lax.all_to_all(triangle, CHIPS, 0, 0, tiled=True).reshape(CH, BLOCK)  6.18 us
    unnamed x26, local copies, waits for them, and re-layouts  3.74 us
    ppermute x1, starting transfers between devices, body(): right_got = lax.ppermute(right, 'core', SWAP)  3.24 us
  transfers between devices with their start and end apart: 4, of which 3 were waited for; matrix products, arithmetic and copies ran while one was open for 3% of the time, Pallas kernels for 1%

profile of v2, /device:TPU:1, one launch (start us, length us, event | category | flops | bytes accessed | tf_op | source)
XLA Modules:
  0.0 116.5 jit_solution(10597019223043603033)
XLA Ops:
  0.0 0.7 convert_element_type.3
  0.7 0.8 broadcast_in_dim.42.wb_ref
  1.6 1.3 %copy-done = f32[48,48,128]{2,1,0:T(8,128)S(1)} copy-done((f32[48,48,128]{2,1,0:T(8,128)S(1)}, f32[48,48,128]{2,1,0:T(8,128)}, u32[]{:S(2)}) %copy-start) | copy-done | bytes 1179672
  2.9 0.9 copy-done.2
  3.8 0.7 copy-done.4
  4.5 0.7 copy-done.6
  5.1 1.5 %shard_map.100 = bf16[2,128,2304]{2,1,0:T(8,128)(2,1)S(1)} custom-call(f32[48,48,128]{2,1,0:T(8,128)S(1)} %copy-done, f32[8,48]{1,0:T(8,128)S(1)} %broadcast_in_dim.33.row_ref, f32[8,48]{1,0:T(8,128)S(1)} %broadcast_in_dim.34.col_ref, f32[1,128]{1,0:T(1,128)S(1)} %bitcast.24, f32[1,128]{1,0:T(1,128)S(1)} %bitcast.26, bf16[128,640]{1,0:T(8,128)(2,1)S(1)} %copy-done.2, ...), custom_call_target="tpu_custom_call" | custom-call | flops 100000000 | bytes 3000000 | tf_op jit(solution)/shard_map/pallas_call | solution.py:205
  6.6 2.2 %copy.22 = bf16[128,2,2304]{2,1,0:T(2,128)(2,1)} copy(bf16[128,2,2304]{2,0,1:T(8,128)(2,1)S(1)} %bitcast.19) | data formatting | bytes 2359296 | tf_op jit(solution)/shard_map/transpose | solution.py:216
  8.9 16.3 %all-to-all-start = ((bf16[128,2,2304]{2,1,0:T(2,128)(2,1)}), bf16[128,2,2304]{2,1,0:T(2,128)(2,1)S(1)}, u32[]{:S(2)}, u32[]{:S(2)}) async-start(bf16[128,2,2304]{2,1,0:T(2,128)(2,1)} %copy.22), calls=%async_computation | async-start | bytes 2359296 | tf_op jit(solution)/shard_map/all_to_all | solution.py:217
  25.2 32.4 %all-to-all-done = bf16[128,2,2304]{2,1,0:T(2,128)(2,1)S(1)} async-done(((bf16[128,2,2304]{2,1,0:T(2,128)(2,1)}), bf16[128,2,2304]{2,1,0:T(2,128)(2,1)S(1)}, u32[]{:S(2)}, u32[]{:S(2)}) %all-to-all-start) | async-done | bytes 1179680 | tf_op jit(solution)/shard_map/all_to_all | solution.py:217
  57.7 1.6 %fusion = (bf16[128,1,2304]{2,1,0:T(2,128)(2,1)S(1)}, bf16[128,1,2304]{2,1,0:T(2,128)(2,1)S(1)}) fusion(bf16[128,2,2304]{2,1,0:T(2,128)(2,1)S(1)} %all-to-all-done), kind=kLoop, calls=%fused_computation.6 | loop fusion | bytes 2359296 | tf_op jit(solution)/shard_map/slice | solution.py:218
  59.4 3.2 %collective-permute-start.1 = (bf16[128,2304]{1,0:T(8,128)(2,1)S(1)}, bf16[128,2304]{1,0:T(8,128)(2,1)S(1)}, u32[]{:S(2)}, u32[]{:S(2)}) collective-permute-start(bf16[128,2304]{1,0:T(8,128)(2,1)S(1)} %bitcast.21), channel_id=1, source_target_pairs={{0,16},{16,0},{1,17},{17,1},{2,18},{18,2},{3,19},{19,3},{4,20},{20... | collective-permute-start | bytes 1769480 | tf_op jit(solution)/shard_map/ppermute | solution.py:223
  62.6 1.2 %constant_dynamic-slice_fusion = (bf16[64,1,2304]{2,1,0:T(2,128)(2,1)S(1)}, bf16[64,1,2304]{2,1,0:T(2,128)(2,1)S(1)}) fusion(bf16[128,1,2304]{2,1,0:T(2,128)(2,1)S(1)} %get-tuple-element.6, s32[]{:T(128)S(6)} %select_n.15, s32[]{:T(128)S(6)} %select_n.14), kind=kLoop, calls=%fused_computation.4 | loop fusion | bytes 1179656 | tf_op jit(solution)/shard_map/dynamic_slice | solution.py:221
  63.9 0.3 collective-permute-start
  64.2 1.5 %collective-permute-done.lg_ref = bf16[64,2304]{1,0:T(8,128)(2,1)S(1)} collective-permute-done((bf16[64,2304]{1,0:T(8,128)(2,1)S(1)}, bf16[64,2304]{1,0:T(8,128)(2,1)S(1)}, u32[]{:S(2)}, u32[]{:S(2)}) %collective-permute-start) | collective-permute-done | bytes 294944 | tf_op jit(solution)/shard_map/ppermute | solution.py:222
  65.7 19.7 %shard_map.101 = bf16[128,2304]{1,0:T(8,128)(2,1)S(1)} custom-call(bf16[64,2304]{1,0:T(8,128)(2,1)S(1)} %bitcast.23, bf16[64,2304]{1,0:T(8,128)(2,1)S(1)} %collective-permute-done.lg_ref, bf16[128,2304]{1,0:T(8,128)(2,1)S(1)} %bitcast.22, bf16[128,2304]{1,0:T(8,128)(2,1)S(1)} %collective-permute-done.1.rg_ref), custom_call_target="tpu_custom_call" | custom-call | flops 100000000 | bytes 3000000 | tf_op jit(solution)/shard_map/pallas_call | solution.py:224
  85.5 0.9 reshape.10
  86.5 6.2 %all-to-all-start.1 = ((bf16[128,2,1152]{2,1,0:T(2,128)(2,1)}), bf16[128,2,1152]{2,1,0:T(2,128)(2,1)S(1)}, u32[]{:S(2)}, u32[]{:S(2)}) async-start(bf16[128,2,1152]{2,1,0:T(2,128)(2,1)} %reshape.10), calls=%async_computation.1 | async-start | bytes 1179648 | tf_op jit(solution)/shard_map/all_to_all | solution.py:238
  92.7 0.8 slice.14.w_ref
  93.6 0.1 copy.26.bias_ref
  93.7 0.7 slice_bitcast_fusion.wb_ref
  94.4 1.0 shard_map.102.gate_ref
  95.4 18.9 %all-to-all-done.1 = bf16[128,2,1152]{2,1,0:T(2,128)(2,1)S(1)} async-done(((bf16[128,2,1152]{2,1,0:T(2,128)(2,1)}), bf16[128,2,1152]{2,1,0:T(2,128)(2,1)S(1)}, u32[]{:S(2)}, u32[]{:S(2)}) %all-to-all-start.1) | async-done | bytes 589856 | tf_op jit(solution)/shard_map/all_to_all | solution.py:238
  114.4 2.1 %shard_map.103 = f32[48,48,128]{2,1,0:T(8,128)} custom-call(bf16[128,2304]{1,0:T(8,128)(2,1)S(1)} %bitcast.20, f32[2304,128]{1,0:T(8,128)S(1)} %shard_map.102.gate_ref, f32[128,1]{1,0:T(8,128)S(1)} %copy.25.gain_ref, f32[128,1]{1,0:T(8,128)S(1)} %copy.26.bias_ref, bf16[128,128]{1,0:T(8,128)(2,1)S(1)} %copy-done.3, f32[1,128]{1,0:T(1,128)S(1)} %bitcast.28), custom_call_target="tpu_custom_call" | custom-call | flops 100000000 | bytes 3000000 | tf_op jit(solution)/shard_map/pallas_call | solution.py:239
  (27 shorter events, 0.5 us)
Async XLA Ops:
  1.6 1.3 %copy-start = (f32[48,48,128]{2,1,0:T(8,128)S(1)}, f32[48,48,128]{2,1,0:T(8,128)}, u32[]{:S(2)}) copy-start(f32[48,48,128]{2,1,0:T(8,128)} %act_ref.3) | copy-start | bytes 3538948
  2.9 0.9 copy-start.2
  3.8 0.7 copy-start.4
  4.5 0.7 copy-start.6
  8.9 48.8 %all-to-all-start = ((bf16[128,2,2304]{2,1,0:T(2,128)(2,1)}), bf16[128,2,2304]{2,1,0:T(2,128)(2,1)S(1)}, u32[]{:S(2)}, u32[]{:S(2)}) async-start(bf16[128,2,2304]{2,1,0:T(2,128)(2,1)} %copy.22), calls=%async_computation | async-start | bytes 2359296 | tf_op jit(solution)/shard_map/all_to_all | solution.py:217
  59.4 6.4 %collective-permute-start.1 = (bf16[128,2304]{1,0:T(8,128)(2,1)S(1)}, bf16[128,2304]{1,0:T(8,128)(2,1)S(1)}, u32[]{:S(2)}, u32[]{:S(2)}) collective-permute-start(bf16[128,2304]{1,0:T(8,128)(2,1)S(1)} %bitcast.21), channel_id=1, source_target_pairs={{0,16},{16,0},{1,17},{17,1},{2,18},{18,2},{3,19},{19,3},{4,20},{20... | collective-permute-start | bytes 1769480 | tf_op jit(solution)/shard_map/ppermute | solution.py:223
  63.9 1.9 %collective-permute-start = (bf16[64,2304]{1,0:T(8,128)(2,1)S(1)}, bf16[64,2304]{1,0:T(8,128)(2,1)S(1)}, u32[]{:S(2)}, u32[]{:S(2)}) collective-permute-start(bf16[64,2304]{1,0:T(8,128)(2,1)S(1)} %bitcast.30), channel_id=1, source_target_pairs={{0,16},{16,0},{1,17},{17,1},{2,18},{18,2},{3,19},{19,3},{4,20},{20... | collective-permute-start | bytes 884744 | tf_op jit(solution)/shard_map/ppermute | solution.py:222
  85.5 8.0 %copy-start.9 = (f32[128]{0:T(128)S(1)}, f32[128]{0:T(128)}, u32[]{:S(2)}) copy-start(f32[128]{0:T(128)} %param.16) | copy-start | bytes 1540
  85.5 8.1 %copy-start.10 = (f32[128]{0:T(128)S(1)}, f32[128]{0:T(128)}, u32[]{:S(2)}) copy-start(f32[128]{0:T(128)} %param.17) | copy-start | bytes 1540
  85.5 8.9 %copy-start.1 = (f32[48,48,128]{2,1,0:T(8,128)S(1)}, f32[48,48,128]{2,1,0:T(8,128)}, u32[]{:S(2)}) copy-start(f32[48,48,128]{2,1,0:T(8,128)} %act_ref.3) | copy-start | bytes 3538948
  85.5 8.9 %copy-start.5 = (f32[128]{0:T(128)S(1)}, f32[128]{0:T(128)}, u32[]{:S(2)}) copy-start(f32[128]{0:T(128)} %param.12) | copy-start | bytes 1540
  85.5 8.8 %copy-start.7 = (f32[128]{0:T(128)S(1)}, f32[128]{0:T(128)}, u32[]{:S(2)}) copy-start(f32[128]{0:T(128)} %param.13) | copy-start | bytes 1540
  86.5 27.8 %all-to-all-start.1 = ((bf16[128,2,1152]{2,1,0:T(2,128)(2,1)}), bf16[128,2,1152]{2,1,0:T(2,128)(2,1)S(1)}, u32[]{:S(2)}, u32[]{:S(2)}) async-start(bf16[128,2,1152]{2,1,0:T(2,128)(2,1)} %reshape.10), calls=%async_computation.1 | async-start | bytes 1179648 | tf_op jit(solution)/shard_map/all_to_all | solution.py:238
  95.3 19.0 %copy-start.3 = (bf16[128,128]{1,0:T(8,128)(2,1)S(1)}, bf16[128,128]{1,0:T(8,128)(2,1)}, u32[]{:S(2)}) copy-start(bf16[128,128]{1,0:T(8,128)(2,1)} %w_ref.3) | copy-start | bytes 98308
  95.4 19.0 %copy-start.8 = (f32[128]{0:T(128)S(1)}, f32[128]{0:T(128)}, u32[]{:S(2)}) copy-start(f32[128]{0:T(128)} %param.19) | copy-start | bytes 1540

commit v3 on v0

v3 whole, which is shorter than its diff:
```python
import jax
import jax.numpy as jnp
from jax import lax
from jax.experimental import pallas as pl
from jax.experimental.pallas import tpu as pltpu
from jax.sharding import Mesh
from jax.sharding import PartitionSpec as P

CH = 128
ROW = ("y_lo", "x", "core")
COL = ("z", "y_hi")
CHIPS = ("y_hi", "z", "y_lo", "x")
SWAP = [(0, 1), (1, 0)]
LANES = 128
SIDE = 48
HALF = SIDE // 2
WIDE = 32
THIN = 16
BLOCK = SIDE * SIDE
SHARE = BLOCK // 2
PIECE = 3 * LANES
F32 = jnp.float32
BF16 = jnp.bfloat16
EPS = 1e-05


def cat(parts, axis):
    return jnp.concatenate(list(parts), axis=axis)


def pieces(residues):
    for width, lo in ((WIDE, 0), (THIN, WIDE)):
        count = LANES // width
        n = residues // count
        for v in range(0, n, 3):
            yield [(b * n + u, lo, width) for u in range(v, v + 3) for b in range(count)]


def sides_kernel(
    act_hbm, mask_hbm, gain_hbm, bias_hbm, w_hbm, wb_hbm,
    out_ref, normed_ref,
    act, mask_v, gain_v, bias_v, w, wb, wt, wbt, sem,
):
    halves = [
        pltpu.make_async_copy(
            act_hbm.at[h * HALF : (h + 1) * HALF], act.at[h * HALF : (h + 1) * HALF], sem.at[h]
        )
        for h in range(2)
    ]
    small = [
        pltpu.make_async_copy(src, dst, sem.at[2 + n])
        for n, (src, dst) in enumerate(
            ((mask_hbm, mask_v), (gain_hbm, gain_v), (bias_hbm, bias_v), (w_hbm, w), (wb_hbm, wb))
        )
    ]
    for copy in halves[:1] + small + halves[1:]:
        copy.start()
    for copy in small:
        copy.wait()
    wt[...] = w[:, : 4 * CH].T
    for n in range(4):
        wbt[n * CH : (n + 1) * CH] = jnp.broadcast_to(wb[:, n * CH : (n + 1) * CH], (CH, LANES)).T
    total = mask_v.shape[1]
    known = jnp.broadcast_to(mask_v[...].astype(F32), (8, total))
    index = lax.broadcasted_iota(jnp.int32, (total, LANES), 0)
    place = lax.broadcasted_iota(jnp.int32, (total, LANES), 1)
    of_axis = []
    for axis in (ROW, COL):
        chosen = index == place + lax.axis_index(axis) * SIDE
        of_axis.append(jnp.dot(known, chosen.astype(F32), preferred_element_type=F32))
    row_mask, col_mask = of_axis
    index = lax.broadcasted_iota(jnp.int32, (LANES, PIECE), 0)
    place = lax.broadcasted_iota(jnp.int32, (LANES, PIECE), 1)
    for h in range(2):
        halves[h].wait()
        for at in range(h * HALF, (h + 1) * HALF, 8):
            values = act[at : at + 8].reshape(8 * SIDE, LANES)
            off = values - jnp.mean(values, axis=-1, keepdims=True)
            spread = jnp.mean(jnp.square(off), axis=-1, keepdims=True)
            normed = off * lax.rsqrt(spread + EPS) * gain_v[...] + bias_v[...]
            normed_ref[at : at + 8] = normed.astype(BF16).reshape(8, SIDE, LANES)
        for n, piece in enumerate(pieces(HALF)):
            rows = cat((normed_ref[h * HALF + k, lo : lo + width] for k, lo, width in piece), 0)
            _, lo, width = piece[0]
            count = LANES // width
            step = HALF // count
            k_of = h * HALF + piece[0][0] + place // LANES + (place % LANES) // width * step
            mask = jnp.dot(row_mask, (index == k_of).astype(F32), preferred_element_type=F32)
            i_of = lo + place % width
            mask = mask * jnp.dot(col_mask, (index == i_of).astype(F32), preferred_element_type=F32)
            for side in range(2):
                at = side * 2 * CH
                both = lax.dot_general(
                    wt[at : at + 2 * CH],
                    rows,
                    (((1,), (1,)), ((), ())),
                    preferred_element_type=F32,
                ) + wbt[at : at + 2 * CH, :1]
                value = mask[:1] * jax.nn.sigmoid(both[:CH]) * both[CH:]
                out_ref[side, h, :, n * PIECE : (n + 1) * PIECE] = value.astype(BF16)


def beside_kernel(normed_ref, w_ref, wb_ref, gate_ref, wide_ref, thin_ref):
    for n, piece in enumerate(pieces(SIDE)):
        rows = cat((normed_ref[k, lo : lo + width] for k, lo, width in piece), 0)
        lin = jnp.dot(rows, w_ref[...], preferred_element_type=F32) + wb_ref[...]
        gate_ref[n * PIECE : (n + 1) * PIECE] = jax.nn.sigmoid(lin)
    for ref, width in ((wide_ref, WIDE), (thin_ref, THIN)):
        count = LANES // width
        size = count * LANES
        lane = lax.broadcasted_iota(jnp.int32, (LANES, size), 1)
        row = lax.broadcasted_iota(jnp.int32, (LANES, 1), 0)
        for g in range(count):
            goes = (row // width * count + g) * width + row % width
            ref[g * LANES : (g + 1) * LANES] = (lane == goes).astype(F32).astype(BF16)


def gather_k(values, blocks, wide, thin, dst_ref, at):
    for width, perm, lanes_at, col_at in (
        (WIDE, wide, 0, 0),
        (THIN, thin, HALF * WIDE, blocks * WIDE),
    ):
        count = LANES // width
        n = HALF // count
        groups = blocks // count
        left = cat(
            (
                cat(
                    (
                        values[
                            (m * count + g) * 16 : (m * count + g + 1) * 16,
                            lanes_at + a * LANES : lanes_at + (a + 1) * LANES,
                        ]
                        for g in range(count)
                    ),
                    1,
                )
                for m in range(groups)
                for a in range(n)
            ),
            0,
        )
        moved = jnp.dot(left, perm[...], preferred_element_type=F32).astype(BF16)
        for m in range(groups):
            for b in range(count):
                dst_ref[
                    at + b * n * 16 : at + (b + 1) * n * 16,
                    col_at + m * LANES : col_at + (m + 1) * LANES,
                ] = moved[m * n * 16 : (m + 1) * n * 16, b * LANES : (b + 1) * LANES]


def triangle_kernel(mine_ref, got_ref, wide, thin, out_ref, left_ref, right_ref, tri_ref):
    start = pl.multiple_of(lax.axis_index("core") * CH, CH)
    for n, ref in enumerate((mine_ref, got_ref)):
        at = n * HALF * 16
        gather_k(ref[0, pl.ds(start, CH), :], 8, wide, thin, left_ref, at)
        gather_k(ref[1], 16, wide, thin, right_ref, at)
    product = lax.dot_general(
        left_ref[...], right_ref[...], (((0,), (0,)), ((), ())), preferred_element_type=F32
    )
    for strip in range(6):
        tri_ref[strip] = product[:, strip * LANES : (strip + 1) * LANES]

    def residue(strip, i):
        if i < WIDE:
            return tri_ref[strip, pl.ds(i, 8, stride=WIDE), :]
        return tri_ref[strip, pl.ds(8 * WIDE + i - WIDE, 8, stride=THIN), :]

    for width, perm, lanes_at, strip_at in (
        (WIDE, wide, 0, 0),
        (THIN, thin, SIDE * WIDE, 4),
    ):
        count = LANES // width
        n = SIDE // count
        groups = 16 // count
        left = cat(
            (
                cat((residue(strip_at + m, b * n + a) for b in range(count)), 1)
                for m in range(groups)
                for a in range(n)
            ),
            0,
        ).astype(BF16)
        moved = jnp.dot(left, perm[...], preferred_element_type=F32)
        for m in range(groups):
            for a in range(n):
                rows = moved[(m * n + a) * 8 : (m * n + a + 1) * 8]
                for g in range(0, count, 2):
                    at = (m * count + g) * 8
                    out_ref[
                        at : at + 16, lanes_at + a * LANES : lanes_at + (a + 1) * LANES
                    ] = cat(
                        (rows[:, g * LANES : (g + 1) * LANES], rows[:, (g + 1) * LANES : (g + 2) * LANES]), 0
                    ).astype(BF16)


def finish_kernel(tri_ref, gate_ref, gain_ref, bias_ref, w_ref, wb_ref, out_ref):
    twice = cat((w_ref[...], w_ref[...]), 0)
    for n, piece in enumerate(pieces(SIDE)):
        tri = tri_ref[:, n * PIECE : (n + 1) * PIECE].astype(F32)
        off = tri - jnp.mean(tri, axis=0, keepdims=True)
        spread = jnp.mean(jnp.square(off), axis=0, keepdims=True)
        mixed = off * lax.rsqrt(spread + EPS) * gain_ref[...] + bias_ref[...]
        high = mixed.astype(BF16)
        low = (mixed - high.astype(F32)).astype(BF16)
        lin = lax.dot_general(
            cat((high, low), 0), twice, (((0,), (0,)), ((), ())), preferred_element_type=F32
        )
        update = gate_ref[n * PIECE : (n + 1) * PIECE] * (lin + wb_ref[...])
        at = 0
        for i, lo, width in piece:
            out_ref[i, lo : lo + width] = update[at : at + width]
            at += width


def call(kernel, outs, scratch=(), in_specs=None, cost=10**9):
    options = {} if in_specs is None else {"in_specs": in_specs}
    return pl.pallas_call(
        kernel,
        out_shape=outs,
        scratch_shapes=scratch,
        compiler_params=pltpu.CompilerParams(vmem_limit_bytes=40 * 2**20),
        cost_estimate=pl.CostEstimate(flops=cost, bytes_accessed=3 * 10**6, transcendentals=0),
        **options,
    )


def body(
    pair_act,
    residue_mask,
    norm_in_gain,
    norm_in_bias,
    proj_in,
    proj_bias,
    norm_out_gain,
    norm_out_bias,
    proj_out,
    out_bias,
):
    shape = jax.ShapeDtypeStruct
    vmem = pltpu.VMEM
    total = residue_mask.shape[0]
    sides, normed = call(
        sides_kernel,
        (shape((2, 2, CH, SHARE), BF16), shape((SIDE, SIDE, CH), BF16)),
        [
            vmem((SIDE, SIDE, CH), F32),
            vmem((1, total), jnp.int32),
            vmem((1, CH), F32),
            vmem((1, CH), F32),
            vmem((CH, 5 * CH), BF16),
            vmem((1, 5 * CH), F32),
            vmem((4 * CH, CH), BF16),
            vmem((4 * CH, LANES), F32),
            pltpu.SemaphoreType.DMA((7,)),
        ],
        [pl.BlockSpec(memory_space=pltpu.HBM)] * 6,
    )(
        pair_act,
        residue_mask[None],
        norm_in_gain[None],
        norm_in_bias[None],
        proj_in,
        proj_bias[None],
    )
    packed = sides.transpose(2, 1, 0, 3).reshape(2 * CH, 2, SHARE)
    packed = lax.all_to_all(packed, CHIPS + ("core",), 0, 0, tiled=True)
    gate, wide, thin = call(
        beside_kernel,
        (shape((BLOCK, CH), F32), shape((512, 512), BF16), shape((1024, 1024), BF16)),
    )(normed, proj_in[:, 4 * CH :], proj_bias[None, 4 * CH :])
    mine = packed.transpose(1, 0, 2)
    got = lax.ppermute(mine, "core", SWAP)
    triangle = call(
        triangle_kernel,
        shape((CH, BLOCK), BF16),
        [
            vmem((16 * SIDE, 8 * SIDE), BF16),
            vmem((16 * SIDE, 16 * SIDE), BF16),
            vmem((6, 8 * SIDE, LANES), F32),
        ],
    )(mine, got, wide, thin)
    triangle = triangle.reshape(CH, 2, BLOCK // 2)
    triangle = lax.all_to_all(triangle, CHIPS, 0, 0, tiled=True).reshape(CH, BLOCK)
    return call(finish_kernel, shape((SIDE, SIDE, CH), F32))(
        triangle, gate, norm_out_gain[:, None], norm_out_bias[:, None], proj_out, out_bias[None]
    )


def solution(mesh):
    fine = Mesh(mesh.devices.reshape(2, 4, 2, 8, 2), ROW + COL)
    return jax.shard_map(
        body,
        mesh=fine,
        in_specs=(P(ROW, COL, None), P(), P(), P(), P(), P(), P(), P(), P(), P()),
        out_specs=P(ROW, COL, None),
        check_vma=False,
    )
```

time: 390 us -> 96.7 us (0.25); the launches traced: 385 us -> 96.3 us
  waiting for transfers between devices: 291 us -> 20.9 us
  blocking collectives: 0 us -> 48.7 us
  local copies, waits for them, and re-layouts: 54.5 us -> 8.16 us
  between operations: 13.5 us -> 0.1 us
  matrix products: 12.8 us -> 0 us
  Pallas kernels: 0 us -> 9.88 us
  other arithmetic: 7.69 us -> 0 us
    all_gather x2 -> x0, waiting for transfers between devices: 290 us -> none  [the longest x1 149 us: body(): left_all = lax.all_gather(left_side, 'col', axis=1, tiled=True)]
    all_to_all x0 -> x1, blocking collectives: none -> 48.7 us  [body(): packed = lax.all_to_all(packed, CHIPS + ('core',), 0, 0, tiled=True)]
    all_gather x2 -> x0, local copies, waits for them, and re-layouts: 27.4 us -> none  [the longest x1 14 us: body(): lax.all_gather(right_side, 'row', axis=0, tiled=True)]
    all_to_all x2 -> x1, local copies, waits for them, and re-layouts: 23.7 us -> 0.12 us  [body(): packed = lax.all_to_all(packed, CHIPS + ('core',), 0, 0, tiled=True)]
    all_to_all x1, waiting for transfers between devices: 0.01 us -> 20.5 us  [body(): lax.all_to_all(triangle, CHIPS, 0, 0, tiled=True).reshape(CH, BLOCK)]
    dot_general x3 -> x0, matrix products: 12.8 us -> none  [the longest x1 8.97 us: body(): jnp.einsum('kic,kjc->ijc', left_panel, lax.all_gather(right_side, 'row',...]
    pallas_call x0 -> x4, Pallas kernels: none -> 9.88 us  [the longest x1 3.63 us: body(): call(triangle_kernel, shape((CH, BLOCK), BF16), [vmem((16 * SIDE, 8 * SID...]
    convert_element_type x3 -> x0, other arithmetic: 4.73 us -> none  [the longest x1 2.19 us: body(): left_side = (pair_mask * jax.nn.sigmoid(projected[:, :, :CH]) * projected...]
  transfers between devices with their start and end apart: 3 -> 2, of which waited for: 2 -> 2; matrix products, arithmetic and copies ran while one was open for 7% -> 1% of each run, Pallas kernels for 0% -> 1%
where the time goes in v3:
time: 96.7 us; the launch traced here: 96.3 us
  blocking collectives  48.7 us (50%)
  waiting for transfers between devices  20.9 us (22%)
  Pallas kernels  9.88 us (10%)
  starting transfers between devices  8.49 us (9%)
  local copies, waits for them, and re-layouts  8.16 us (8%)
    all_to_all x1, blocking collectives, body(): packed = lax.all_to_all(packed, CHIPS + ('core',), 0, 0, tiled=True)  48.7 us
    all_to_all x1, waiting for transfers between devices, body(): lax.all_to_all(triangle, CHIPS, 0, 0, tiled=True).reshape(CH, BLOCK)  20.5 us
    all_to_all x1, starting transfers between devices, body(): lax.all_to_all(triangle, CHIPS, 0, 0, tiled=True).reshape(CH, BLOCK)  7.15 us
    pallas_call x1, Pallas kernels, body(): call(triangle_kernel, shape((CH, BLOCK), BF16), [vmem((16 * SIDE, 8 * SID...  3.63 us
    unnamed x17, local copies, waits for them, and re-layouts  3.58 us
    pallas_call x1, Pallas kernels, body(): call(sides_kernel, (shape((2, 2, CH, SHARE), BF16), shape((SIDE, SIDE, CH...  2.82 us
    pallas_call x1, Pallas kernels, body(): call(finish_kernel, shape((SIDE, SIDE, CH), F32))  2.09 us
  transfers between devices with their start and end apart: 2, of which 2 were waited for; matrix products, arithmetic and copies ran while one was open for 1% of the time, Pallas kernels for 1%

profile of v3, /device:TPU:1, one launch (start us, length us, event | category | flops | bytes accessed | tf_op | source)
XLA Modules:
  0.0 96.3 jit_solution(15293418824560484807)
XLA Ops:
  0.0 0.7 broadcast_in_dim.24.mask_hbm
  0.7 0.7 broadcast_in_dim.27.wb_hbm
  1.4 0.9 copy-done
  2.3 1.3 %copy-done.1 = f32[48,48,128]{2,1,0:T(8,128)S(1)} copy-done((f32[48,48,128]{2,1,0:T(8,128)S(1)}, f32[48,48,128]{2,1,0:T(8,128)}, u32[]{:S(2)}) %copy-start.1) | copy-done | bytes 1179672
  3.6 0.7 copy-done.3
  4.2 0.7 copy-done.4
  4.9 2.8 %shard_map.100 = (bf16[2,2,128,1152]{3,2,1,0:T(8,128)(2,1)S(1)}, bf16[48,48,128]{2,1,0:T(8,128)(2,1)S(1)}) custom-call(f32[48,48,128]{2,1,0:T(8,128)S(1)} %copy-done.1, s32[1,768]{1,0:T(1,128)S(1)} %broadcast_in_dim.24.mask_hbm, f32[1,128]{1,0:T(1,128)S(1)} %bitcast.18, f32[1,128]{1,0:T(1,128)S(1)} %bitcast.19, bf16[128,640]{1,0:T(8,128)(2,1)S(1)} %copy-done, ...), custom_call_target="tpu_custom_call" | custom-call | flops 1000000000 | bytes 3000000 | tf_op jit(solution)/shard_map/pallas_call | solution.py:243
  7.7 1.2 %copy.17 = bf16[128,2,2,1152]{3,2,1,0:T(2,128)(2,1)S(1)} copy(bf16[128,2,2,1152]{3,0,1,2:T(8,128)(2,1)S(1)} %bitcast.16) | data formatting | bytes 2359296 | tf_op jit(solution)/shard_map/transpose | solution.py:266
  8.9 48.7 %all_to_all.10 = bf16[256,2,1152]{2,1,0:T(2,128)(2,1)S(1)} all-to-all(bf16[256,2,1152]{2,1,0:T(2,128)(2,1)S(1)} %bitcast.21), channel_id=1, replica_groups=mesh['y_lo'=2,'x'=4,'core'=2,'z'=8,'y_hi'=2] {'y_hi','z','y_lo','x','core'}, dimensions={0} | all-to-all | bytes 2359296 | tf_op jit(solution)/shard_map/all_to_all | solution.py:267
  57.7 0.1 copy.23
  57.8 1.3 %collective-permute-start = (bf16[2,256,1152]{2,1,0:T(8,128)(2,1)S(1)}, bf16[2,256,1152]{2,1,0:T(8,128)(2,1)S(1)}, u32[]{:S(2)}, u32[]{:S(2)}) collective-permute-start(bf16[2,256,1152]{2,1,0:T(8,128)(2,1)S(1)} %bitcast.14), channel_id=1, source_target_pairs={{0,16},{16,0},{1,17},{17,1},{2,18},{18,2},{3,19},{19,3},{4,20},{20... | collective-permute-start | bytes 3538952 | tf_op jit(solution)/shard_map/ppermute | solution.py:273
  59.1 0.7 slice_bitcast_fusion.wb_ref
  59.8 1.3 %shard_map.101 = (f32[2304,128]{1,0:T(8,128)S(1)}, bf16[512,512]{1,0:T(8,128)(2,1)S(1)}, bf16[1024,1024]{1,0:T(8,128)(2,1)S(1)}) custom-call(bf16[48,48,128]{2,1,0:T(8,128)(2,1)S(1)} %get-tuple-element.11.normed_ref, bf16[128,128]{1,0:T(8,128)(2,1)S(1)} %slice.6.w_ref, f32[1,128]{1,0:T(1,128)S(1)} %slice_bitcast_fusion.wb_ref), custom_call_target="tpu_custom_call" | custom-call | flops 1000000000 | bytes 3000000 | tf_op jit(solution)/shard_map/pallas_call | solution.py:268
  61.2 0.4 collective-permute-done.got_ref
  61.6 3.6 %shard_map.102 = bf16[128,2304]{1,0:T(8,128)(2,1)S(1)} custom-call(bf16[2,256,1152]{2,1,0:T(8,128)(2,1)S(1)} %bitcast.15, bf16[2,256,1152]{2,1,0:T(8,128)(2,1)S(1)} %collective-permute-done.got_ref, bf16[512,512]{1,0:T(8,128)(2,1)S(1)} %get-tuple-element.12.wide, bf16[1024,1024]{1,0:T(8,128)(2,1)S(1)} %get-tuple-element.13.thin), custom_call_target="tpu_custom_call" | custom-call | flops 1000000000 | bytes 3000000 | tf_op jit(solution)/shard_map/pallas_call | solution.py:274
  65.2 0.0 copy-start.6
  65.2 0.0 copy-start.7
  65.3 0.9 reshape.10
  66.2 7.2 %all-to-all-start.1 = ((bf16[128,2,1152]{2,1,0:T(2,128)(2,1)}), bf16[128,2,1152]{2,1,0:T(2,128)(2,1)S(1)}, u32[]{:S(2)}, u32[]{:S(2)}) async-start(bf16[128,2,1152]{2,1,0:T(2,128)(2,1)} %reshape.10), calls=%async_computation.1 | async-start | bytes 1179648 | tf_op jit(solution)/shard_map/all_to_all | solution.py:284
  73.4 0.1 copy.19.gain_ref
  73.5 0.1 copy.20.bias_ref
  73.6 20.5 %all-to-all-done.1 = bf16[128,2,1152]{2,1,0:T(2,128)(2,1)S(1)} async-done(((bf16[128,2,1152]{2,1,0:T(2,128)(2,1)}), bf16[128,2,1152]{2,1,0:T(2,128)(2,1)S(1)}, u32[]{:S(2)}, u32[]{:S(2)}) %all-to-all-start.1) | async-done | bytes 589856 | tf_op jit(solution)/shard_map/all_to_all | solution.py:284
  94.1 0.1 copy.21
  94.2 2.1 %shard_map.103 = f32[48,48,128]{2,1,0:T(8,128)} custom-call(bf16[128,2304]{1,0:T(8,128)(2,1)S(1)} %bitcast.17, f32[2304,128]{1,0:T(8,128)S(1)} %get-tuple-element.14.gate_ref, f32[128,1]{1,0:T(8,128)S(1)} %copy.19.gain_ref, f32[128,1]{1,0:T(8,128)S(1)} %copy.20.bias_ref, bf16[128,128]{1,0:T(8,128)(2,1)S(1)} %copy-done.2, f32[1,128]{1,0:T(1,128)S(1)} %bitcast.20), custom_call_target="tpu_custom_call" | custom-call | flops 1000000000 | bytes 3000000 | tf_op jit(solution)/shard_map/pallas_call | solution.py:285
  (11 shorter events, 0.0 us)
Async XLA Ops:
  1.4 0.9 copy-start
  2.3 1.3 %copy-start.1 = (f32[48,48,128]{2,1,0:T(8,128)S(1)}, f32[48,48,128]{2,1,0:T(8,128)}, u32[]{:S(2)}) copy-start(f32[48,48,128]{2,1,0:T(8,128)} %act_hbm.1) | copy-start | bytes 3538948
  3.6 0.7 copy-start.3
  4.2 0.7 copy-start.4
  57.8 3.8 %collective-permute-start = (bf16[2,256,1152]{2,1,0:T(8,128)(2,1)S(1)}, bf16[2,256,1152]{2,1,0:T(8,128)(2,1)S(1)}, u32[]{:S(2)}, u32[]{:S(2)}) collective-permute-start(bf16[2,256,1152]{2,1,0:T(8,128)(2,1)S(1)} %bitcast.14), channel_id=1, source_target_pairs={{0,16},{16,0},{1,17},{17,1},{2,18},{18,2},{3,19},{19,3},{4,20},{20... | collective-permute-start | bytes 3538952 | tf_op jit(solution)/shard_map/ppermute | solution.py:273
  65.2 8.1 %copy-start.6 = (f32[128]{0:T(128)S(1)}, f32[128]{0:T(128)}, u32[]{:S(2)}) copy-start(f32[128]{0:T(128)} %param.16) | copy-start | bytes 1540
  65.2 8.3 %copy-start.7 = (f32[128]{0:T(128)S(1)}, f32[128]{0:T(128)}, u32[]{:S(2)}) copy-start(f32[128]{0:T(128)} %param.17) | copy-start | bytes 1540
  66.2 28.0 %copy-start.2 = (bf16[128,128]{1,0:T(8,128)(2,1)S(1)}, bf16[128,128]{1,0:T(8,128)(2,1)}, u32[]{:S(2)}) copy-start(bf16[128,128]{1,0:T(8,128)(2,1)} %w_ref.1) | copy-start | bytes 98308
  66.2 28.0 %copy-start.5 = (f32[128]{0:T(128)S(1)}, f32[128]{0:T(128)}, u32[]{:S(2)}) copy-start(f32[128]{0:T(128)} %param.19) | copy-start | bytes 1540
  66.2 27.9 %all-to-all-start.1 = ((bf16[128,2,1152]{2,1,0:T(2,128)(2,1)}), bf16[128,2,1152]{2,1,0:T(2,128)(2,1)S(1)}, u32[]{:S(2)}, u32[]{:S(2)}) async-start(bf16[128,2,1152]{2,1,0:T(2,128)(2,1)} %reshape.10), calls=%async_computation.1 | async-start | bytes 1179648 | tf_op jit(solution)/shard_map/all_to_all | solution.py:284

commit v4 on v3

--- a/solution.py
+++ b/solution.py
@@ -38,7 +38,7 @@
 
 def sides_kernel(
     act_hbm, mask_hbm, gain_hbm, bias_hbm, w_hbm, wb_hbm,
-    out_ref, normed_ref,
+    out_ref, normed_ref, gate_w_ref, gate_b_ref,
     act, mask_v, gain_v, bias_v, w, wb, wt, wbt, sem,
 ):
     halves = [
@@ -50,7 +50,7 @@
     small = [
         pltpu.make_async_copy(src, dst, sem.at[2 + n])
         for n, (src, dst) in enumerate(
-            ((mask_hbm, mask_v), (gain_hbm, gain_v), (bias_hbm, bias_v), (w_hbm, w), (wb_hbm, wb))
+            ((mask_hbm, mask_v.at[0]), (gain_hbm, gain_v.at[0]), (bias_hbm, bias_v.at[0]), (w_hbm, w), (wb_hbm, wb.at[0]))
         )
     ]
     for copy in halves[:1] + small + halves[1:]:
@@ -58,6 +58,8 @@
     for copy in small:
         copy.wait()
     wt[...] = w[:, : 4 * CH].T
+    gate_w_ref[...] = w[:, 4 * CH :]
+    gate_b_ref[...] = jnp.broadcast_to(wb[:, 4 * CH :], gate_b_ref.shape)
     for n in range(4):
         wbt[n * CH : (n + 1) * CH] = jnp.broadcast_to(wb[:, n * CH : (n + 1) * CH], (CH, LANES)).T
     total = mask_v.shape[1]
@@ -100,21 +102,6 @@
                 out_ref[side, h, :, n * PIECE : (n + 1) * PIECE] = value.astype(BF16)
 
 
-def beside_kernel(normed_ref, w_ref, wb_ref, gate_ref, wide_ref, thin_ref):
-    for n, piece in enumerate(pieces(SIDE)):
-        rows = cat((normed_ref[k, lo : lo + width] for k, lo, width in piece), 0)
-        lin = jnp.dot(rows, w_ref[...], preferred_element_type=F32) + wb_ref[...]
-        gate_ref[n * PIECE : (n + 1) * PIECE] = jax.nn.sigmoid(lin)
-    for ref, width in ((wide_ref, WIDE), (thin_ref, THIN)):
-        count = LANES // width
-        size = count * LANES
-        lane = lax.broadcasted_iota(jnp.int32, (LANES, size), 1)
-        row = lax.broadcasted_iota(jnp.int32, (LANES, 1), 0)
-        for g in range(count):
-            goes = (row // width * count + g) * width + row % width
-            ref[g * LANES : (g + 1) * LANES] = (lane == goes).astype(F32).astype(BF16)
-
-
 def gather_k(values, blocks, wide, thin, dst_ref, at):
     for width, perm, lanes_at, col_at in (
         (WIDE, wide, 0, 0),
@@ -149,12 +136,62 @@
                 ] = moved[m * n * 16 : (m + 1) * n * 16, b * LANES : (b + 1) * LANES]
 
 
-def triangle_kernel(mine_ref, got_ref, wide, thin, out_ref, left_ref, right_ref, tri_ref):
+def gather_sides(ref, wide, thin, left_ref, right_ref, at):
     start = pl.multiple_of(lax.axis_index("core") * CH, CH)
-    for n, ref in enumerate((mine_ref, got_ref)):
-        at = n * HALF * 16
-        gather_k(ref[0, pl.ds(start, CH), :], 8, wide, thin, left_ref, at)
-        gather_k(ref[1], 16, wide, thin, right_ref, at)
+    gather_k(ref[0, pl.ds(start, CH), :], 8, wide, thin, left_ref, at)
+    gather_k(ref[1], 16, wide, thin, right_ref, at)
+
+
+def build_permutations(wide_ref, thin_ref):
+    for ref, width in ((wide_ref, WIDE), (thin_ref, THIN)):
+        count = LANES // width
+        size = count * LANES
+        lane = lax.broadcasted_iota(jnp.int32, (LANES, size), 1)
+        row = lax.broadcasted_iota(jnp.int32, (LANES, 1), 0)
+        for g in range(count):
+            goes = (row // width * count + g) * width + row % width
+            ref[g * LANES : (g + 1) * LANES] = (lane == goes).astype(F32).astype(BF16)
+
+
+def beside_kernel(
+    mine_ref, normed_ref, w_ref, wb_ref, gain_hbm, bias_hbm, out_w_hbm, out_b_hbm,
+    left_ref, right_ref, gate_ref, wide_ref, thin_ref, gain_ref, bias_ref, twice_ref, out_b_ref,
+    gain_v, bias_v, out_b_v, sem,
+):
+    copies = [
+        pltpu.make_async_copy(src, dst, sem.at[n])
+        for n, (src, dst) in enumerate(
+            (
+                (gain_hbm, gain_v.at[0]),
+                (bias_hbm, bias_v.at[0]),
+                (out_b_hbm, out_b_v.at[0]),
+                (out_w_hbm, twice_ref.at[:CH]),
+                (out_w_hbm, twice_ref.at[CH:]),
+            )
+        )
+    ]
+    for copy in copies:
+        copy.start()
+    build_permutations(wide_ref, thin_ref)
+    gather_sides(mine_ref, wide_ref, thin_ref, left_ref, right_ref, 0)
+    for n, piece in enumerate(pieces(SIDE)):
+        rows = cat((normed_ref[k, lo : lo + width] for k, lo, width in piece), 0)
+        lin = jnp.dot(rows, w_ref[...], preferred_element_type=F32) + wb_ref[:1]
+        gate_ref[n * PIECE : (n + 1) * PIECE] = jax.nn.sigmoid(lin)
+    for copy in copies:
+        copy.wait()
+    gain_ref[...] = jnp.broadcast_to(gain_v[...], (CH, LANES)).T
+    bias_ref[...] = jnp.broadcast_to(bias_v[...], (CH, LANES)).T
+    out_b_ref[...] = jnp.broadcast_to(out_b_v[...], out_b_ref.shape)
+
+
+def triangle_kernel(
+    left_mine, right_mine, got_ref, wide, thin, out_ref, left_ref, right_ref, tri_ref
+):
+    own = HALF * 16
+    left_ref[:own] = left_mine[...]
+    right_ref[:own] = right_mine[...]
+    gather_sides(got_ref, wide, thin, left_ref, right_ref, own)
     product = lax.dot_general(
         left_ref[...], right_ref[...], (((0,), (0,)), ((), ())), preferred_element_type=F32
     )
@@ -187,34 +224,43 @@
                 rows = moved[(m * n + a) * 8 : (m * n + a + 1) * 8]
                 for g in range(0, count, 2):
                     at = (m * count + g) * 8
-                    out_ref[
-                        at : at + 16, lanes_at + a * LANES : lanes_at + (a + 1) * LANES
-                    ] = cat(
-                        (rows[:, g * LANES : (g + 1) * LANES], rows[:, (g + 1) * LANES : (g + 2) * LANES]), 0
-                    ).astype(BF16)
-
-
-def finish_kernel(tri_ref, gate_ref, gain_ref, bias_ref, w_ref, wb_ref, out_ref):
-    twice = cat((w_ref[...], w_ref[...]), 0)
+                    two = cat(
+                        (rows[:, (g + d) * LANES : (g + d + 1) * LANES] for d in range(2)), 0
+                    )
+                    half, lane = divmod(lanes_at + a * LANES, SHARE)
+                    out_ref[half, at : at + 16, lane : lane + LANES] = two.astype(BF16)
+
+
+def finish_kernel(tri_ref, gate_ref, gain_ref, bias_ref, twice_ref, wb_ref, out_hbm, out, sem):
+    copies = []
     for n, piece in enumerate(pieces(SIDE)):
-        tri = tri_ref[:, n * PIECE : (n + 1) * PIECE].astype(F32)
+        half, lane = divmod(n * PIECE, SHARE)
+        tri = tri_ref[half, :, lane : lane + PIECE].astype(F32)
         off = tri - jnp.mean(tri, axis=0, keepdims=True)
         spread = jnp.mean(jnp.square(off), axis=0, keepdims=True)
-        mixed = off * lax.rsqrt(spread + EPS) * gain_ref[...] + bias_ref[...]
+        mixed = off * lax.rsqrt(spread + EPS) * gain_ref[:, :1] + bias_ref[:, :1]
         high = mixed.astype(BF16)
         low = (mixed - high.astype(F32)).astype(BF16)
         lin = lax.dot_general(
-            cat((high, low), 0), twice, (((0,), (0,)), ((), ())), preferred_element_type=F32
-        )
-        update = gate_ref[n * PIECE : (n + 1) * PIECE] * (lin + wb_ref[...])
-        at = 0
-        for i, lo, width in piece:
-            out_ref[i, lo : lo + width] = update[at : at + width]
-            at += width
-
-
-def call(kernel, outs, scratch=(), in_specs=None, cost=10**9):
-    options = {} if in_specs is None else {"in_specs": in_specs}
+            cat((high, low), 0),
+            twice_ref[...],
+            (((0,), (0,)), ((), ())),
+            preferred_element_type=F32,
+        )
+        update = gate_ref[n * PIECE : (n + 1) * PIECE] * (lin + wb_ref[:1])
+        for at, (i, lo, width) in enumerate(piece):
+            out[i, lo : lo + width] = update[at * width : (at + 1) * width]
+        count = len(piece) // 3
+        for i, lo, width in piece[:count]:
+            where = (slice(i, i + 3), slice(lo, lo + width))
+            copy = pltpu.make_async_copy(out.at[where], out_hbm.at[where], sem.at[len(copies)])
+            copy.start()
+            copies.append(copy)
+    for copy in copies:
+        copy.wait()
+
+
+def call(kernel, outs, scratch=(), cost=10**9, **options):
     return pl.pallas_call(
         kernel,
         out_shape=outs,
@@ -223,6 +269,10 @@
         cost_estimate=pl.CostEstimate(flops=cost, bytes_accessed=3 * 10**6, transcendentals=0),
         **options,
     )
+
+
+def stay(arrays):
+    return [pltpu.with_memory_space_constraint(x, pltpu.HBM) for x in arrays]
 
 
 def body(
@@ -240,9 +290,15 @@
     shape = jax.ShapeDtypeStruct
     vmem = pltpu.VMEM
     total = residue_mask.shape[0]
-    sides, normed = call(
+    hbm, here = pl.BlockSpec(memory_space=pltpu.HBM), pl.BlockSpec(memory_space=vmem)
+    sides, normed, gate_w, gate_b = call(
         sides_kernel,
-        (shape((2, 2, CH, SHARE), BF16), shape((SIDE, SIDE, CH), BF16)),
+        (
+            shape((2, 2, CH, SHARE), BF16),
+            shape((SIDE, SIDE, CH), BF16),
+            shape((CH, CH), BF16),
+            shape((8, CH), F32),
+        ),
         [
             vmem((SIDE, SIDE, CH), F32),
             vmem((1, total), jnp.int32),
@@ -254,37 +310,44 @@
             vmem((4 * CH, LANES), F32),
             pltpu.SemaphoreType.DMA((7,)),
         ],
-        [pl.BlockSpec(memory_space=pltpu.HBM)] * 6,
-    )(
-        pair_act,
-        residue_mask[None],
-        norm_in_gain[None],
-        norm_in_bias[None],
-        proj_in,
-        proj_bias[None],
-    )
+        in_specs=[hbm] * 6,
+    )(*stay((pair_act, residue_mask, norm_in_gain, norm_in_bias, proj_in, proj_bias)))
     packed = sides.transpose(2, 1, 0, 3).reshape(2 * CH, 2, SHARE)
     packed = lax.all_to_all(packed, CHIPS + ("core",), 0, 0, tiled=True)
-    gate, wide, thin = call(
-        beside_kernel,
-        (shape((BLOCK, CH), F32), shape((512, 512), BF16), shape((1024, 1024), BF16)),
-    )(normed, proj_in[:, 4 * CH :], proj_bias[None, 4 * CH :])
     mine = packed.transpose(1, 0, 2)
     got = lax.ppermute(mine, "core", SWAP)
+    left, right, gate, wide, thin, *last = call(
+        beside_kernel,
+        (
+            shape((8 * SIDE, 8 * SIDE), BF16),
+            shape((8 * SIDE, 16 * SIDE), BF16),
+            shape((BLOCK, CH), F32),
+            shape((512, 512), BF16),
+            shape((1024, 1024), BF16),
+            shape((CH, LANES), F32),
+            shape((CH, LANES), F32),
+            shape((2 * CH, CH), BF16),
+            shape((8, CH), F32),
+        ),
+        [vmem((1, CH), F32)] * 3 + [pltpu.SemaphoreType.DMA((5,))],
+        in_specs=[here] * 4 + [hbm] * 4,
+    )(mine, normed, gate_w, gate_b, *stay((norm_out_gain, norm_out_bias, proj_out, out_bias)))
     triangle = call(
         triangle_kernel,
-        shape((CH, BLOCK), BF16),
+        shape((2, CH, SHARE), BF16),
         [
             vmem((16 * SIDE, 8 * SIDE), BF16),
             vmem((16 * SIDE, 16 * SIDE), BF16),
             vmem((6, 8 * SIDE, LANES), F32),
         ],
-    )(mine, got, wide, thin)
-    triangle = triangle.reshape(CH, 2, BLOCK // 2)
-    triangle = lax.all_to_all(triangle, CHIPS, 0, 0, tiled=True).reshape(CH, BLOCK)
-    return call(finish_kernel, shape((SIDE, SIDE, CH), F32))(
-        triangle, gate, norm_out_gain[:, None], norm_out_bias[:, None], proj_out, out_bias[None]
-    )
+    )(left, right, got, wide, thin)
+    triangle = lax.all_to_all(triangle.transpose(1, 0, 2), CHIPS, 0, 0, tiled=True)
+    return call(
+        finish_kernel,
+        shape((SIDE, SIDE, CH), F32),
+        [vmem((SIDE, SIDE, CH), F32), pltpu.SemaphoreType.DMA((32,))],
+        out_specs=hbm,
+    )(triangle.transpose(1, 0, 2), gate, *last)
 
 
 def solution(mesh):

time: 96.7 us -> 90.5 us (0.936)
  blocking collectives: 48.7 us -> 76.3 us
  waiting for transfers between devices: 20.9 us -> 0.68 us
  starting transfers between devices: 8.49 us -> 1.33 us
  local copies, waits for them, and re-layouts: 8.16 us -> 2.01 us
    all_to_all x0 -> x1, blocking collectives: none -> 27.6 us  [body(): lax.all_to_all(triangle.transpose(1, 0, 2), CHIPS, 0, 0, tiled=True)]
    all_to_all x1 -> x0, waiting for transfers between devices: 20.5 us -> none  [body(): lax.all_to_all(triangle, CHIPS, 0, 0, tiled=True).reshape(CH, BLOCK)]
    all_to_all x1 -> x0, starting transfers between devices: 7.15 us -> none  [body(): lax.all_to_all(triangle, CHIPS, 0, 0, tiled=True).reshape(CH, BLOCK)]
    unnamed x17 -> x0, local copies, waits for them, and re-layouts: 3.58 us -> none
    broadcast_in_dim x5 -> x0, local copies, waits for them, and re-layouts: 2.29 us -> none  [the longest x1 0.69 us: body(): residue_mask[None]]
  transfers between devices with their start and end apart: 2 -> 1, of which waited for: 2 -> 1; matrix products, arithmetic and copies ran while one was open for 1% -> 0% of each run, Pallas kernels for 1% -> 2%
where the time goes in v4:
time: 90.5 us; the launch traced here: 90.4 us
  blocking collectives  76.3 us (84%)
  Pallas kernels  10 us (11%)
  local copies, waits for them, and re-layouts  2.01 us (2%)
  starting transfers between devices  1.33 us (1%)
    all_to_all x1, blocking collectives, body(): packed = lax.all_to_all(packed, CHIPS + ('core',), 0, 0, tiled=True)  48.7 us
    all_to_all x1, blocking collectives, body(): lax.all_to_all(triangle.transpose(1, 0, 2), CHIPS, 0, 0, tiled=True)  27.6 us
    pallas_call x1, Pallas kernels, body(): call(sides_kernel, (shape((2, 2, CH, SHARE), BF16), shape((SIDE, SIDE, CH...  3.51 us
    pallas_call x1, Pallas kernels, body(): call(triangle_kernel, shape((2, CH, SHARE), BF16), [vmem((16 * SIDE, 8 *...  2.68 us
    pallas_call x1, Pallas kernels, body(): call(finish_kernel, shape((SIDE, SIDE, CH), F32), [vmem((SIDE, SIDE, CH),...  2.05 us
  transfers between devices with their start and end apart: 1, of which 1 were waited for; matrix products, arithmetic and copies ran while one was open for 0% of the time, Pallas kernels for 2%

profile of v4, /device:TPU:1, one launch (start us, length us, event | category | flops | bytes accessed | tf_op | source)
XLA Modules:
  0.0 90.4 jit_solution(12670026059997511365)
XLA Ops:
  0.0 3.5 %shard_map.100 = (bf16[2,2,128,1152]{3,2,1,0:T(8,128)(2,1)S(1)}, bf16[48,48,128]{2,1,0:T(8,128)(2,1)S(1)}, bf16[128,128]{1,0:T(8,128)(2,1)S(1)}, f32[8,128]{1,0:T(8,128)S(1)}) custom-call(f32[48,48,128]{2,1,0:T(8,128)} %act_hbm.1, s32[768]{0:T(1024)} %mask_hbm.1, f32[128]{0:T(128)} %gain_hbm.2, f32[128]{0:T(128)} %bias_hbm.2, bf16[128,640]{1,0:T(8,128)(2,1)} %w_hbm.1, ...), custom_call_target="tpu_custom_call" | custom-call | flops 1000000000 | bytes 3000000 | tf_op jit(solution)/shard_map/pallas_call | solution.py:294
  3.5 1.2 %copy.15 = bf16[128,2,2,1152]{3,2,1,0:T(2,128)(2,1)S(1)} copy(bf16[128,2,2,1152]{3,0,1,2:T(8,128)(2,1)S(1)} %bitcast.12) | data formatting | bytes 2359296 | tf_op jit(solution)/shard_map/transpose | solution.py:315
  4.7 48.7 %all_to_all.10 = bf16[256,2,1152]{2,1,0:T(2,128)(2,1)S(1)} all-to-all(bf16[256,2,1152]{2,1,0:T(2,128)(2,1)S(1)} %bitcast.14), channel_id=1, replica_groups=mesh['y_lo'=2,'x'=4,'core'=2,'z'=8,'y_hi'=2] {'y_hi','z','y_lo','x','core'}, dimensions={0} | all-to-all | bytes 2359296 | tf_op jit(solution)/shard_map/all_to_all | solution.py:316
  53.5 0.1 copy.21
  53.6 1.3 %collective-permute-start = (bf16[2,256,1152]{2,1,0:T(8,128)(2,1)S(1)}, bf16[2,256,1152]{2,1,0:T(8,128)(2,1)S(1)}, u32[]{:S(2)}, u32[]{:S(2)}) collective-permute-start(bf16[2,256,1152]{2,1,0:T(8,128)(2,1)S(1)} %bitcast.10), channel_id=1, source_target_pairs={{0,16},{16,0},{1,17},{17,1},{2,18},{18,2},{3,19},{19,3},{4,20},{20... | collective-permute-start | bytes 3538952 | tf_op jit(solution)/shard_map/ppermute | solution.py:318
  54.9 1.8 %shard_map.101 = (bf16[384,384]{1,0:T(8,128)(2,1)S(1)}, bf16[384,768]{1,0:T(8,128)(2,1)S(1)}, f32[2304,128]{1,0:T(8,128)S(1)}, bf16[512,512]{1,0:T(8,128)(2,1)S(...) custom-call(bf16[2,256,1152]{2,1,0:T(8,128)(2,1)S(1)} %bitcast.11, ...), custom_call_target="tpu_custom_call" | custom-call | flops 1000000000 | bytes 3000000 | tf_op jit(solution)/shard_map/pallas_call | solution.py:319
  56.7 0.7 collective-permute-done.got_ref
  57.4 2.7 %shard_map.102 = bf16[2,128,1152]{2,1,0:T(8,128)(2,1)S(1)} custom-call(bf16[384,384]{1,0:T(8,128)(2,1)S(1)} %get-tuple-element.22.left_mine, bf16[384,768]{1,0:T(8,128)(2,1)S(1)} %get-tuple-element.23.right_mine, bf16[2,256,1152]{2,1,0:T(8,128)(2,1)S(1)} %collective-permute-done.got_ref, bf16[512,512]{1,0:T(8,128)(2,1)S(1)} %get-tuple-element.24.wide, ...), custom_call_target="tpu_custom_call" | custom-call | flops 1000000000 | bytes 3000000 | tf_op jit(solution)/shard_map/pallas_call | solution.py:335
  60.1 0.6 copy.17
  60.7 27.6 %all_to_all.11 = bf16[128,2,1152]{2,1,0:T(2,128)(2,1)S(1)} all-to-all(bf16[128,2,1152]{2,1,0:T(2,128)(2,1)S(1)} %copy.17), channel_id=1, replica_groups=mesh['y_lo'=2,'x'=4,'core'=2,'z'=8,'y_hi'=2] {'y_hi','z','y_lo','x'}, dimensions={0} | all-to-all | bytes 1179648 | tf_op jit(solution)/shard_map/all_to_all | solution.py:344
  88.3 0.1 copy.22
  88.3 2.1 %shard_map.103 = f32[48,48,128]{2,1,0:T(8,128)} custom-call(bf16[2,128,1152]{2,1,0:T(8,128)(2,1)S(1)} %bitcast.13, f32[2304,128]{1,0:T(8,128)S(1)} %get-tuple-element.26.gate_ref, f32[128,128]{1,0:T(8,128)S(1)} %get-tuple-element.27.gain_ref, f32[128,128]{1,0:T(8,128)S(1)} %get-tuple-element.28.bias_ref, bf16[256,128]{1,0:T(8,128)(2,1)S(1)} %get-tuple-element.29.twice_ref, ...), custom_call_target="tpu_custom_call" | custom-call | flops 1000000000 | bytes 3000000 | tf_op jit(solution)/shard_map/pallas_call | solution.py:345
Async XLA Ops:
  53.6 3.8 %collective-permute-start = (bf16[2,256,1152]{2,1,0:T(8,128)(2,1)S(1)}, bf16[2,256,1152]{2,1,0:T(8,128)(2,1)S(1)}, u32[]{:S(2)}, u32[]{:S(2)}) collective-permute-start(bf16[2,256,1152]{2,1,0:T(8,128)(2,1)S(1)} %bitcast.10), channel_id=1, source_target_pairs={{0,16},{16,0},{1,17},{17,1},{2,18},{18,2},{3,19},{19,3},{4,20},{20... | collective-permute-start | bytes 3538952 | tf_op jit(solution)/shard_map/ppermute | solution.py:318

commit v5 on v4

--- a/solution.py
+++ b/solution.py
@@ -9,7 +9,9 @@
 CH = 128
 ROW = ("y_lo", "x", "core")
 COL = ("z", "y_hi")
-CHIPS = ("y_hi", "z", "y_lo", "x")
+ALL = ROW + COL
+TURN = (3, 6, 0, 5, 1, 7, 2, 4)
+HALVES = (1, 0)
 SWAP = [(0, 1), (1, 0)]
 LANES = 128
 SIDE = 48
@@ -39,7 +41,7 @@
 def sides_kernel(
     act_hbm, mask_hbm, gain_hbm, bias_hbm, w_hbm, wb_hbm,
     out_ref, normed_ref, gate_w_ref, gate_b_ref,
-    act, mask_v, gain_v, bias_v, w, wb, wt, wbt, sem,
+    act, mask_v, gain_v, bias_v, w, wb, wt32, wt, wbt, sem,
 ):
     halves = [
         pltpu.make_async_copy(
@@ -57,11 +59,15 @@
         copy.start()
     for copy in small:
         copy.wait()
-    wt[...] = w[:, : 4 * CH].T
+    for n in range(4):
+        side, kind = divmod(n, 2)
+        cols = slice(n * CH, (n + 1) * CH)
+        rows = pl.ds(kind * 2 * CH + side, CH, stride=2)
+        wt32[rows, :] = w[:, cols].astype(F32).T
+        wbt[rows, :] = jnp.broadcast_to(wb[:, cols], (CH, LANES)).T
+    wt[...] = wt32[...].astype(BF16)
     gate_w_ref[...] = w[:, 4 * CH :]
     gate_b_ref[...] = jnp.broadcast_to(wb[:, 4 * CH :], gate_b_ref.shape)
-    for n in range(4):
-        wbt[n * CH : (n + 1) * CH] = jnp.broadcast_to(wb[:, n * CH : (n + 1) * CH], (CH, LANES)).T
     total = mask_v.shape[1]
     known = jnp.broadcast_to(mask_v[...].astype(F32), (8, total))
     index = lax.broadcasted_iota(jnp.int32, (total, LANES), 0)
@@ -81,41 +87,42 @@
             spread = jnp.mean(jnp.square(off), axis=-1, keepdims=True)
             normed = off * lax.rsqrt(spread + EPS) * gain_v[...] + bias_v[...]
             normed_ref[at : at + 8] = normed.astype(BF16).reshape(8, SIDE, LANES)
-        for n, piece in enumerate(pieces(HALF)):
-            rows = cat((normed_ref[h * HALF + k, lo : lo + width] for k, lo, width in piece), 0)
-            _, lo, width = piece[0]
-            count = LANES // width
-            step = HALF // count
-            k_of = h * HALF + piece[0][0] + place // LANES + (place % LANES) // width * step
-            mask = jnp.dot(row_mask, (index == k_of).astype(F32), preferred_element_type=F32)
-            i_of = lo + place % width
-            mask = mask * jnp.dot(col_mask, (index == i_of).astype(F32), preferred_element_type=F32)
-            for side in range(2):
-                at = side * 2 * CH
-                both = lax.dot_general(
-                    wt[at : at + 2 * CH],
-                    rows,
-                    (((1,), (1,)), ((), ())),
-                    preferred_element_type=F32,
-                ) + wbt[at : at + 2 * CH, :1]
-                value = mask[:1] * jax.nn.sigmoid(both[:CH]) * both[CH:]
-                out_ref[side, h, :, n * PIECE : (n + 1) * PIECE] = value.astype(BF16)
-
-
-def gather_k(values, blocks, wide, thin, dst_ref, at):
+    for n, piece in enumerate(pieces(SIDE)):
+        rows = cat((normed_ref[k, lo : lo + width] for k, lo, width in piece), 0)
+        _, lo, width = piece[0]
+        step = SIDE * width // LANES
+        k_of = piece[0][0] + place // LANES + (place % LANES) // width * step
+        mask = jnp.dot(row_mask, (index == k_of).astype(F32), preferred_element_type=F32)
+        i_of = lo + place % width
+        mask = mask * jnp.dot(col_mask, (index == i_of).astype(F32), preferred_element_type=F32)
+        gate, value = (
+            lax.dot_general(
+                wt[at : at + 2 * CH],
+                rows,
+                (((1,), (1,)), ((), ())),
+                preferred_element_type=F32,
+            )
+            + wbt[at : at + 2 * CH, :1]
+            for at in (0, 2 * CH)
+        )
+        value = mask[:1] * jax.nn.sigmoid(gate) * value
+        out_ref[:, n * PIECE : (n + 1) * PIECE] = value.astype(BF16)
+
+
+def gather_k(values, blocks, wide, thin, dst_ref):
     for width, perm, lanes_at, col_at in (
         (WIDE, wide, 0, 0),
-        (THIN, thin, HALF * WIDE, blocks * WIDE),
+        (THIN, thin, SIDE * WIDE, blocks * WIDE),
     ):
         count = LANES // width
-        n = HALF // count
+        n = SIDE // count
         groups = blocks // count
         left = cat(
             (
                 cat(
                     (
                         values[
-                            (m * count + g) * 16 : (m * count + g + 1) * 16,
+                            (m * count + g) * 8 : (m * count + g + 1) * 8,
                             lanes_at + a * LANES : lanes_at + (a + 1) * LANES,
                         ]
                         for g in range(count)
@@ -126,20 +133,24 @@
                 for a in range(n)
             ),
             0,
-        )
+        ).astype(BF16)
         moved = jnp.dot(left, perm[...], preferred_element_type=F32).astype(BF16)
         for m in range(groups):
             for b in range(count):
                 dst_ref[
-                    at + b * n * 16 : at + (b + 1) * n * 16,
+                    b * n * 8 : (b + 1) * n * 8,
                     col_at + m * LANES : col_at + (m + 1) * LANES,
-                ] = moved[m * n * 16 : (m + 1) * n * 16, b * LANES : (b + 1) * LANES]
-
-
-def gather_sides(ref, wide, thin, left_ref, right_ref, at):
-    start = pl.multiple_of(lax.axis_index("core") * CH, CH)
-    gather_k(ref[0, pl.ds(start, CH), :], 8, wide, thin, left_ref, at)
-    gather_k(ref[1], 16, wide, thin, right_ref, at)
+                ] = moved[m * n * 8 : (m + 1) * n * 8, b * LANES : (b + 1) * LANES]
+
+
+def product(ref, wide, thin, left_ref, right_ref):
+    core, half = lax.axis_index("core"), CH // 2
+    start = pl.multiple_of((core if HALVES[0] == 0 else 1 - core) * half, half)
+    gather_k(ref[0, pl.ds(start, half), :].astype(F32), 8, wide, thin, left_ref)
+    gather_k(ref[1].astype(F32), 16, wide, thin, right_ref)
+    return lax.dot_general(
+        left_ref[...], right_ref[...], (((0,), (0,)), ((), ())), preferred_element_type=F32
+    )
 
 
 def build_permutations(wide_ref, thin_ref):
@@ -155,8 +166,8 @@
 
 def beside_kernel(
     mine_ref, normed_ref, w_ref, wb_ref, gain_hbm, bias_hbm, out_w_hbm, out_b_hbm,
-    left_ref, right_ref, gate_ref, wide_ref, thin_ref, gain_ref, bias_ref, twice_ref, out_b_ref,
-    gain_v, bias_v, out_b_v, sem,
+    part_ref, gate_ref, wide_ref, thin_ref, gain_ref, bias_ref, twice_ref, out_b_ref,
+    left_ref, right_ref, gain_v, bias_v, out_b_v, sem,
 ):
     copies = [
         pltpu.make_async_copy(src, dst, sem.at[n])
@@ -173,7 +184,7 @@
     for copy in copies:
         copy.start()
     build_permutations(wide_ref, thin_ref)
-    gather_sides(mine_ref, wide_ref, thin_ref, left_ref, right_ref, 0)
+    part_ref[...] = product(mine_ref, wide_ref, thin_ref, left_ref, right_ref)
     for n, piece in enumerate(pieces(SIDE)):
         rows = cat((normed_ref[k, lo : lo + width] for k, lo, width in piece), 0)
         lin = jnp.dot(rows, w_ref[...], preferred_element_type=F32) + wb_ref[:1]
@@ -185,18 +196,10 @@
     out_b_ref[...] = jnp.broadcast_to(out_b_v[...], out_b_ref.shape)
 
 
-def triangle_kernel(
-    left_mine, right_mine, got_ref, wide, thin, out_ref, left_ref, right_ref, tri_ref
-):
-    own = HALF * 16
-    left_ref[:own] = left_mine[...]
-    right_ref[:own] = right_mine[...]
-    gather_sides(got_ref, wide, thin, left_ref, right_ref, own)
-    product = lax.dot_general(
-        left_ref[...], right_ref[...], (((0,), (0,)), ((), ())), preferred_element_type=F32
-    )
+def triangle_kernel(part_ref, got_ref, wide, thin, out_ref, left_ref, right_ref, tri_ref, out):
+    total = part_ref[...] + product(got_ref, wide, thin, left_ref, right_ref)
     for strip in range(6):
-        tri_ref[strip] = product[:, strip * LANES : (strip + 1) * LANES]
+        tri_ref[strip] = total[:, strip * LANES : (strip + 1) * LANES]
 
     def residue(strip, i):
         if i < WIDE:
@@ -222,13 +225,12 @@
         for m in range(groups):
             for a in range(n):
                 rows = moved[(m * n + a) * 8 : (m * n + a + 1) * 8]
-                for g in range(0, count, 2):
-                    at = (m * count + g) * 8
-                    two = cat(
-                        (rows[:, (g + d) * LANES : (g + d + 1) * LANES] for d in range(2)), 0
-                    )
-                    half, lane = divmod(lanes_at + a * LANES, SHARE)
-                    out_ref[half, at : at + 16, lane : lane + LANES] = two.astype(BF16)
+                half, lane = divmod(lanes_at + a * LANES, SHARE)
+                for g in range(count):
+                    to = pl.ds((m * count + g) * 16 + half, 8, stride=2)
+                    out[lane // LANES, to, :] = rows[:, g * LANES : (g + 1) * LANES]
+    for strip in range(SHARE // LANES):
+        out_ref[:, strip * LANES : (strip + 1) * LANES] = out[strip].astype(BF16)
 
 
 def finish_kernel(tri_ref, gate_ref, gain_ref, bias_ref, twice_ref, wb_ref, out_hbm, out, sem):
@@ -269,6 +271,16 @@
         cost_estimate=pl.CostEstimate(flops=cost, bytes_accessed=3 * 10**6, transcendentals=0),
         **options,
     )
+
+
+def groups():
+    chips = [
+        [(pair * 2 + core) * 16 + z * 2 + y_hi for core in range(2)]
+        for y_hi in HALVES
+        for z in TURN
+        for pair in TURN
+    ]
+    return [[chip[core] for chip in chips] for core in range(2)]
 
 
 def stay(arrays):
@@ -294,7 +306,7 @@
     sides, normed, gate_w, gate_b = call(
         sides_kernel,
         (
-            shape((2, 2, CH, SHARE), BF16),
+            shape((2 * CH, BLOCK), BF16),
             shape((SIDE, SIDE, CH), BF16),
             shape((CH, CH), BF16),
             shape((8, CH), F32),
@@ -306,21 +318,22 @@
             vmem((1, CH), F32),
             vmem((CH, 5 * CH), BF16),
             vmem((1, 5 * CH), F32),
+            vmem((4 * CH, CH), F32),
             vmem((4 * CH, CH), BF16),
             vmem((4 * CH, LANES), F32),
             pltpu.SemaphoreType.DMA((7,)),
         ],
         in_specs=[hbm] * 6,
     )(*stay((pair_act, residue_mask, norm_in_gain, norm_in_bias, proj_in, proj_bias)))
-    packed = sides.transpose(2, 1, 0, 3).reshape(2 * CH, 2, SHARE)
-    packed = lax.all_to_all(packed, CHIPS + ("core",), 0, 0, tiled=True)
+    packed = sides.reshape(CH, 2, BLOCK)
+    packed = lax.all_to_all(packed, ALL, 0, 0, axis_index_groups=groups(), tiled=True)
     mine = packed.transpose(1, 0, 2)
     got = lax.ppermute(mine, "core", SWAP)
-    left, right, gate, wide, thin, *last = call(
+    operands = [vmem((8 * SIDE, 8 * SIDE), BF16), vmem((8 * SIDE, 16 * SIDE), BF16)]
+    part, gate, wide, thin, *last = call(
         beside_kernel,
         (
-            shape((8 * SIDE, 8 * SIDE), BF16),
-            shape((8 * SIDE, 16 * SIDE), BF16),
+            shape((8 * SIDE, 16 * SIDE), F32),
             shape((BLOCK, CH), F32),
             shape((512, 512), BF16),
             shape((1024, 1024), BF16),
@@ -329,19 +342,18 @@
             shape((2 * CH, CH), BF16),
             shape((8, CH), F32),
         ),
-        [vmem((1, CH), F32)] * 3 + [pltpu.SemaphoreType.DMA((5,))],
+        [*operands, *[vmem((1, CH), F32)] * 3, pltpu.SemaphoreType.DMA((5,))],
         in_specs=[here] * 4 + [hbm] * 4,
     )(mine, normed, gate_w, gate_b, *stay((norm_out_gain, norm_out_bias, proj_out, out_bias)))
     triangle = call(
         triangle_kernel,
-        shape((2, CH, SHARE), BF16),
-        [
-            vmem((16 * SIDE, 8 * SIDE), BF16),
-            vmem((16 * SIDE, 16 * SIDE), BF16),
-            vmem((6, 8 * SIDE, LANES), F32),
-        ],
-    )(left, right, got, wide, thin)
-    triangle = lax.all_to_all(triangle.transpose(1, 0, 2), CHIPS, 0, 0, tiled=True)
+        shape((2 * CH, SHARE), BF16),
+        [*operands, vmem((6, 8 * SIDE, LANES), F32), vmem((SHARE // LANES, 2 * CH, LANES), F32)],
+    )(part, got, wide, thin)
+    triangle = triangle.reshape(CH, 2, SHARE)
+    triangle = lax.all_to_all(
+        triangle, ALL, 0, 0, axis_index_groups=groups(), tiled=True
+    )
     return call(
         finish_kernel,
         shape((SIDE, SIDE, CH), F32),

time: 90.5 us -> 86.1 us (0.951)
  blocking collectives: 76.3 us -> 71.8 us
  local copies, waits for them, and re-layouts: 2.01 us -> 0.89 us
  starting transfers between devices: 1.33 us -> 2.39 us
    all_to_all x2, blocking collectives: 76.3 us -> 71.8 us  [the longest x1 45.8 us: body(): lax.all_to_all(packed, ALL, 0, 0, axis_index_groups=groups(), tiled=True)]
    transpose x2 -> x0, local copies, waits for them, and re-layouts: 1.82 us -> none  [the longest x1 1.21 us: body(): packed = sides.transpose(2, 1, 0, 3).reshape(2 * CH, 2, SHARE)]
    ppermute x1, starting transfers between devices: 1.33 us -> 2.39 us  [body(): got = lax.ppermute(mine, 'core', SWAP)]
  transfers between devices with their start and end apart: 1 -> 1, of which waited for: 1 -> 0; matrix products, arithmetic and copies ran while one was open for 0% -> 0% of each run, Pallas kernels for 2% -> 3%
where the time goes in v5:
time: 86.1 us; the launch traced here: 85.8 us
  blocking collectives  71.8 us (83%)
  Pallas kernels  10.6 us (12%)
  starting transfers between devices  2.39 us (3%)
  local copies, waits for them, and re-layouts  0.89 us (1%)
    all_to_all x1, blocking collectives, body(): lax.all_to_all(packed, ALL, 0, 0, axis_index_groups=groups(), tiled=True)  45.8 us
    all_to_all x1, blocking collectives, body(): lax.all_to_all(triangle, ALL, 0, 0, axis_index_groups=groups(), tiled=True)  26 us
    pallas_call x1, Pallas kernels, body(): call(sides_kernel, (shape((2 * CH, BLOCK), BF16), shape((SIDE, SIDE, CH),...  3.34 us
    pallas_call x1, Pallas kernels, body(): call(beside_kernel, (shape((8 * SIDE, 16 * SIDE), F32), shape((BLOCK, CH)...  2.72 us
    pallas_call x1, Pallas kernels, body(): call(triangle_kernel, shape((2 * CH, SHARE), BF16), [*operands, vmem((6,...  2.51 us
    ppermute x1, starting transfers between devices, body(): got = lax.ppermute(mine, 'core', SWAP)  2.39 us
    pallas_call x1, Pallas kernels, body(): call(finish_kernel, shape((SIDE, SIDE, CH), F32), [vmem((SIDE, SIDE, CH),...  2.05 us
  transfers between devices with their start and end apart: 1, of which 0 were waited for; matrix products, arithmetic and copies ran while one was open for 0% of the time, Pallas kernels for 3%

profile of v5, /device:TPU:1, one launch (start us, length us, event | category | flops | bytes accessed | tf_op | source)
XLA Modules:
  0.0 85.8 jit_solution(753955632064313577)
XLA Ops:
  0.0 3.3 %shard_map.100 = (bf16[256,2304]{1,0:T(8,128)(2,1)S(1)}, bf16[48,48,128]{2,1,0:T(8,128)(2,1)S(1)}, bf16[128,128]{1,0:T(8,128)(2,1)S(1)}, f32[8,128]{1,0:T(8,128)S(1)}) custom-call(f32[48,48,128]{2,1,0:T(8,128)} %act_hbm.1, s32[768]{0:T(1024)} %mask_hbm.1, f32[128]{0:T(128)} %gain_hbm.2, f32[128]{0:T(128)} %bias_hbm.2, bf16[128,640]{1,0:T(8,128)(2,1)} %w_hbm.1, ...), custom_call_target="tpu_custom_call" | custom-call | flops 1000000000 | bytes 3000000 | tf_op jit(solution)/shard_map/pallas_call | solution.py:306
  3.3 0.5 reshape.6
  3.8 45.8 %all_to_all.10 = bf16[128,2,2304]{2,1,0:T(2,128)(2,1)S(1)} all-to-all(bf16[128,2,2304]{2,1,0:T(2,128)(2,1)S(1)} %reshape.6), channel_id=1, replica_groups={{103,199,7,167,39,231,71,135,109,205,13,173,45,237,77,141,97,193,1,161,..., dimensions={0} | all-to-all | bytes 2359296 | tf_op jit(solution)/shard_map/all_to_all | solution.py:329
  49.7 0.1 copy.17
  49.8 2.4 %collective-permute-start = (bf16[2,128,2304]{2,1,0:T(8,128)(2,1)S(1)}, bf16[2,128,2304]{2,1,0:T(8,128)(2,1)S(1)}, u32[]{:S(2)}, u32[]{:S(2)}) collective-permute-start(bf16[2,128,2304]{2,1,0:T(8,128)(2,1)S(1)} %bitcast.6), channel_id=1, source_target_pairs={{0,16},{16,0},{1,17},{17,1},{2,18},{18,2},{3,19},{19,3},{4,20},{20... | collective-permute-start | bytes 3538952 | tf_op jit(solution)/shard_map/ppermute | solution.py:331
  52.2 2.7 %shard_map.101 = (f32[384,768]{1,0:T(8,128)S(1)}, f32[2304,128]{1,0:T(8,128)S(1)}, bf16[512,512]{1,0:T(8,128)(2,1)S(1)}, bf16[1024,1024]{1,0:T(8,128)(2,1)S(1)},...) custom-call(bf16[2,128,2304]{2,1,0:T(8,128)(2,1)S(1)} %bitcast.7, ...), custom_call_target="tpu_custom_call" | custom-call | flops 1000000000 | bytes 3000000 | tf_op jit(solution)/shard_map/pallas_call | solution.py:333
  54.9 0.0 collective-permute-done.got_ref
  54.9 2.5 %shard_map.102 = bf16[256,1152]{1,0:T(8,128)(2,1)S(1)} custom-call(f32[384,768]{1,0:T(8,128)S(1)} %get-tuple-element.21.part_ref, bf16[2,128,2304]{2,1,0:T(8,128)(2,1)S(1)} %collective-permute-done.got_ref, bf16[512,512]{1,0:T(8,128)(2,1)S(1)} %get-tuple-element.22.wide, bf16[1024,1024]{1,0:T(8,128)(2,1)S(1)} %get-tuple-element.23.thin), custom_call_target="tpu_custom_call" | custom-call | flops 1000000000 | bytes 3000000 | tf_op jit(solution)/shard_map/pallas_call | solution.py:348
  57.5 0.2 reshape.7
  57.7 26.0 %all_to_all.11 = bf16[128,2,1152]{2,1,0:T(2,128)(2,1)S(1)} all-to-all(bf16[128,2,1152]{2,1,0:T(2,128)(2,1)S(1)} %reshape.7), channel_id=1, replica_groups={{103,199,7,167,39,231,71,135,109,205,13,173,45,237,77,141,97,193,1,161,..., dimensions={0} | all-to-all | bytes 1179648 | tf_op jit(solution)/shard_map/all_to_all | solution.py:354
  83.7 0.1 copy.18
  83.8 2.1 %shard_map.103 = f32[48,48,128]{2,1,0:T(8,128)} custom-call(bf16[2,128,1152]{2,1,0:T(8,128)(2,1)S(1)} %bitcast.8, f32[2304,128]{1,0:T(8,128)S(1)} %get-tuple-element.24.gate_ref, f32[128,128]{1,0:T(8,128)S(1)} %get-tuple-element.25.gain_ref, f32[128,128]{1,0:T(8,128)S(1)} %get-tuple-element.26.bias_ref, bf16[256,128]{1,0:T(8,128)(2,1)S(1)} %get-tuple-element.27.twice_ref, ...), custom_call_target="tpu_custom_call" | custom-call | flops 1000000000 | bytes 3000000 | tf_op jit(solution)/shard_map/pallas_call | solution.py:357
Async XLA Ops:
  49.8 5.1 %collective-permute-start = (bf16[2,128,2304]{2,1,0:T(8,128)(2,1)S(1)}, bf16[2,128,2304]{2,1,0:T(8,128)(2,1)S(1)}, u32[]{:S(2)}, u32[]{:S(2)}) collective-permute-start(bf16[2,128,2304]{2,1,0:T(8,128)(2,1)S(1)} %bitcast.6), channel_id=1, source_target_pairs={{0,16},{16,0},{1,17},{17,1},{2,18},{18,2},{3,19},{19,3},{4,20},{20... | collective-permute-start | bytes 3538952 | tf_op jit(solution)/shard_map/ppermute | solution.py:331

commit v6 on v5

--- a/solution.py
+++ b/solution.py
@@ -10,7 +10,8 @@
 ROW = ("y_lo", "x", "core")
 COL = ("z", "y_hi")
 ALL = ROW + COL
-TURN = (3, 6, 0, 5, 1, 7, 2, 4)
+TURN = (6, 3, 1, 0, 7, 2, 5, 4)
+PAIRS = (6, 3, 1, 0, 7, 2, 5, 4)
 HALVES = (1, 0)
 SWAP = [(0, 1), (1, 0)]
 LANES = 128
@@ -28,6 +29,10 @@
 
 def cat(parts, axis):
     return jnp.concatenate(list(parts), axis=axis)
+
+
+def across(column):
+    return cat([column] * (PIECE // LANES), 1)
 
 
 def pieces(residues):
@@ -102,14 +107,15 @@
                 (((1,), (1,)), ((), ())),
                 preferred_element_type=F32,
             )
-            + wbt[at : at + 2 * CH, :1]
+            + across(wbt[at : at + 2 * CH])
             for at in (0, 2 * CH)
         )
         value = mask[:1] * jax.nn.sigmoid(gate) * value
         out_ref[:, n * PIECE : (n + 1) * PIECE] = value.astype(BF16)
 
 
-def gather_k(values, blocks, wide, thin, dst_ref):
+def gather_k(values, order, wide, thin, dst_ref):
+    blocks = len(order)
     for width, perm, lanes_at, col_at in (
         (WIDE, wide, 0, 0),
         (THIN, thin, SIDE * WIDE, blocks * WIDE),
@@ -122,7 +128,7 @@
                 cat(
                     (
                         values[
-                            (m * count + g) * 8 : (m * count + g + 1) * 8,
+                            order[m * count + g] * 8 : (order[m * count + g] + 1) * 8,
                             lanes_at + a * LANES : lanes_at + (a + 1) * LANES,
                         ]
                         for g in range(count)
@@ -146,8 +152,8 @@
 def product(ref, wide, thin, left_ref, right_ref):
     core, half = lax.axis_index("core"), CH // 2
     start = pl.multiple_of((core if HALVES[0] == 0 else 1 - core) * half, half)
-    gather_k(ref[0, pl.ds(start, half), :].astype(F32), 8, wide, thin, left_ref)
-    gather_k(ref[1].astype(F32), 16, wide, thin, right_ref)
+    gather_k(ref[0, pl.ds(start, half), :].astype(F32), [TURN.index(z) for z in PAIRS], wide, thin, left_ref)
+    gather_k(ref[1].astype(F32), range(16), wide, thin, right_ref)
     return lax.dot_general(
         left_ref[...], right_ref[...], (((0,), (0,)), ((), ())), preferred_element_type=F32
     )
@@ -240,7 +246,7 @@
         tri = tri_ref[half, :, lane : lane + PIECE].astype(F32)
         off = tri - jnp.mean(tri, axis=0, keepdims=True)
         spread = jnp.mean(jnp.square(off), axis=0, keepdims=True)
-        mixed = off * lax.rsqrt(spread + EPS) * gain_ref[:, :1] + bias_ref[:, :1]
+        mixed = off * lax.rsqrt(spread + EPS) * across(gain_ref[...]) + across(bias_ref[...])
         high = mixed.astype(BF16)
         low = (mixed - high.astype(F32)).astype(BF16)
         lin = lax.dot_general(
@@ -278,7 +284,7 @@
         [(pair * 2 + core) * 16 + z * 2 + y_hi for core in range(2)]
         for y_hi in HALVES
         for z in TURN
-        for pair in TURN
+        for pair in PAIRS
     ]
     return [[chip[core] for chip in chips] for core in range(2)]
 

time: 86.1 us -> 83.5 us (0.970)
  blocking collectives: 71.8 us -> 69.2 us
    all_to_all x1, blocking collectives: 45.8 us -> 43.1 us  [body(): lax.all_to_all(packed, ALL, 0, 0, axis_index_groups=groups(), tiled=True)]
where the time goes in v6:
time: 83.5 us; the launch traced here: 83.2 us
  blocking collectives  69.2 us (83%)
  Pallas kernels  10.2 us (12%)
  starting transfers between devices  2.86 us (3%)
  local copies, waits for them, and re-layouts  0.89 us (1%)
    all_to_all x1, blocking collectives, body(): lax.all_to_all(packed, ALL, 0, 0, axis_index_groups=groups(), tiled=True)  43.1 us
    all_to_all x1, blocking collectives, body(): lax.all_to_all(triangle, ALL, 0, 0, axis_index_groups=groups(), tiled=True)  26.1 us
    pallas_call x1, Pallas kernels, body(): call(sides_kernel, (shape((2 * CH, BLOCK), BF16), shape((SIDE, SIDE, CH),...  3.22 us
    ppermute x1, starting transfers between devices, body(): got = lax.ppermute(mine, 'core', SWAP)  2.86 us
    pallas_call x1, Pallas kernels, body(): call(beside_kernel, (shape((8 * SIDE, 16 * SIDE), F32), shape((BLOCK, CH)...  2.71 us
    pallas_call x1, Pallas kernels, body(): call(triangle_kernel, shape((2 * CH, SHARE), BF16), [*operands, vmem((6,...  2.51 us
    pallas_call x1, Pallas kernels, body(): call(finish_kernel, shape((SIDE, SIDE, CH), F32), [vmem((SIDE, SIDE, CH),...  1.8 us
  transfers between devices with their start and end apart: 1, of which 0 were waited for; matrix products, arithmetic and copies ran while one was open for 0% of the time, Pallas kernels for 3%

profile of v6, /device:TPU:1, one launch (start us, length us, event | category | flops | bytes accessed | tf_op | source)
XLA Modules:
  0.0 83.2 jit_solution(14159157491541214710)
XLA Ops:
  0.0 3.2 %shard_map.100 = (bf16[256,2304]{1,0:T(8,128)(2,1)S(1)}, bf16[48,48,128]{2,1,0:T(8,128)(2,1)S(1)}, bf16[128,128]{1,0:T(8,128)(2,1)S(1)}, f32[8,128]{1,0:T(8,128)S(1)}) custom-call(f32[48,48,128]{2,1,0:T(8,128)} %act_hbm.1, s32[768]{0:T(1024)} %mask_hbm.1, f32[128]{0:T(128)} %gain_hbm.2, f32[128]{0:T(128)} %bias_hbm.2, bf16[128,640]{1,0:T(8,128)(2,1)} %w_hbm.1, ...), custom_call_target="tpu_custom_call" | custom-call | flops 1000000000 | bytes 3000000 | tf_op jit(solution)/shard_map/pallas_call | solution.py:312
  3.2 0.5 reshape.6
  3.7 43.1 %all_to_all.10 = bf16[128,2,2304]{2,1,0:T(2,128)(2,1)S(1)} all-to-all(bf16[128,2,2304]{2,1,0:T(2,128)(2,1)S(1)} %reshape.6), channel_id=1, replica_groups={{205,109,45,13,237,77,173,141,199,103,39,7,231,71,167,135,195,99,35,3,2..., dimensions={0} | all-to-all | bytes 2359296 | tf_op jit(solution)/shard_map/all_to_all | solution.py:335
  46.8 0.1 copy.17
  47.0 2.9 %collective-permute-start = (bf16[2,128,2304]{2,1,0:T(8,128)(2,1)S(1)}, bf16[2,128,2304]{2,1,0:T(8,128)(2,1)S(1)}, u32[]{:S(2)}, u32[]{:S(2)}) collective-permute-start(bf16[2,128,2304]{2,1,0:T(8,128)(2,1)S(1)} %bitcast.6), channel_id=1, source_target_pairs={{0,16},{16,0},{1,17},{17,1},{2,18},{18,2},{3,19},{19,3},{4,20},{20... | collective-permute-start | bytes 3538952 | tf_op jit(solution)/shard_map/ppermute | solution.py:337
  49.8 2.7 %shard_map.101 = (f32[384,768]{1,0:T(8,128)S(1)}, f32[2304,128]{1,0:T(8,128)S(1)}, bf16[512,512]{1,0:T(8,128)(2,1)S(1)}, bf16[1024,1024]{1,0:T(8,128)(2,1)S(1)},...) custom-call(bf16[2,128,2304]{2,1,0:T(8,128)(2,1)S(1)} %bitcast.7, ...), custom_call_target="tpu_custom_call" | custom-call | flops 1000000000 | bytes 3000000 | tf_op jit(solution)/shard_map/pallas_call | solution.py:339
  52.5 0.0 collective-permute-done.got_ref
  52.6 2.5 %shard_map.102 = bf16[256,1152]{1,0:T(8,128)(2,1)S(1)} custom-call(f32[384,768]{1,0:T(8,128)S(1)} %get-tuple-element.21.part_ref, bf16[2,128,2304]{2,1,0:T(8,128)(2,1)S(1)} %collective-permute-done.got_ref, bf16[512,512]{1,0:T(8,128)(2,1)S(1)} %get-tuple-element.22.wide, bf16[1024,1024]{1,0:T(8,128)(2,1)S(1)} %get-tuple-element.23.thin), custom_call_target="tpu_custom_call" | custom-call | flops 1000000000 | bytes 3000000 | tf_op jit(solution)/shard_map/pallas_call | solution.py:354
  55.1 0.2 reshape.7
  55.3 26.1 %all_to_all.11 = bf16[128,2,1152]{2,1,0:T(2,128)(2,1)S(1)} all-to-all(bf16[128,2,1152]{2,1,0:T(2,128)(2,1)S(1)} %reshape.7), channel_id=1, replica_groups={{205,109,45,13,237,77,173,141,199,103,39,7,231,71,167,135,195,99,35,3,2..., dimensions={0} | all-to-all | bytes 1179648 | tf_op jit(solution)/shard_map/all_to_all | solution.py:360
  81.4 0.1 copy.18
  81.4 1.8 %shard_map.103 = f32[48,48,128]{2,1,0:T(8,128)} custom-call(bf16[2,128,1152]{2,1,0:T(8,128)(2,1)S(1)} %bitcast.8, f32[2304,128]{1,0:T(8,128)S(1)} %get-tuple-element.24.gate_ref, f32[128,128]{1,0:T(8,128)S(1)} %get-tuple-element.25.gain_ref, f32[128,128]{1,0:T(8,128)S(1)} %get-tuple-element.26.bias_ref, bf16[256,128]{1,0:T(8,128)(2,1)S(1)} %get-tuple-element.27.twice_ref, ...), custom_call_target="tpu_custom_call" | custom-call | flops 1000000000 | bytes 3000000 | tf_op jit(solution)/shard_map/pallas_call | solution.py:363
Async XLA Ops:
  47.0 5.6 %collective-permute-start = (bf16[2,128,2304]{2,1,0:T(8,128)(2,1)S(1)}, bf16[2,128,2304]{2,1,0:T(8,128)(2,1)S(1)}, u32[]{:S(2)}, u32[]{:S(2)}) collective-permute-start(bf16[2,128,2304]{2,1,0:T(8,128)(2,1)S(1)} %bitcast.6), channel_id=1, source_target_pairs={{0,16},{16,0},{1,17},{17,1},{2,18},{18,2},{3,19},{19,3},{4,20},{20... | collective-permute-start | bytes 3538952 | tf_op jit(solution)/shard_map/ppermute | solution.py:337

commit v7 on v6

--- a/solution.py
+++ b/solution.py
@@ -11,7 +11,7 @@
 COL = ("z", "y_hi")
 ALL = ROW + COL
 TURN = (6, 3, 1, 0, 7, 2, 5, 4)
-PAIRS = (6, 3, 1, 0, 7, 2, 5, 4)
+PAIRS = (3, 1, 5, 4, 0, 6, 7, 2)
 HALVES = (1, 0)
 SWAP = [(0, 1), (1, 0)]
 LANES = 128
@@ -57,13 +57,27 @@
     small = [
         pltpu.make_async_copy(src, dst, sem.at[2 + n])
         for n, (src, dst) in enumerate(
-            ((mask_hbm, mask_v.at[0]), (gain_hbm, gain_v.at[0]), (bias_hbm, bias_v.at[0]), (w_hbm, w), (wb_hbm, wb.at[0]))
+            (
+                (mask_hbm, mask_v.at[0]),
+                (gain_hbm, gain_v.at[0]),
+                (bias_hbm, bias_v.at[0]),
+                (w_hbm, w),
+                (wb_hbm, wb.at[0]),
+            )
         )
     ]
     for copy in halves[:1] + small + halves[1:]:
         copy.start()
+    total = mask_v.shape[1]
+    index = lax.broadcasted_iota(jnp.int32, (total, LANES), 0)
+    place = lax.broadcasted_iota(jnp.int32, (total, LANES), 1)
+    chosen = [(index == place + lax.axis_index(axis) * SIDE).astype(F32) for axis in (ROW, COL)]
     for copy in small:
         copy.wait()
+    known = jnp.broadcast_to(mask_v[...].astype(F32), (8, total))
+    row_mask, col_mask = (
+        jnp.dot(known, one, preferred_element_type=F32)[:, :SIDE] for one in chosen
+    )
     for n in range(4):
         side, kind = divmod(n, 2)
         cols = slice(n * CH, (n + 1) * CH)
@@ -73,17 +87,8 @@
     wt[...] = wt32[...].astype(BF16)
     gate_w_ref[...] = w[:, 4 * CH :]
     gate_b_ref[...] = jnp.broadcast_to(wb[:, 4 * CH :], gate_b_ref.shape)
-    total = mask_v.shape[1]
-    known = jnp.broadcast_to(mask_v[...].astype(F32), (8, total))
-    index = lax.broadcasted_iota(jnp.int32, (total, LANES), 0)
-    place = lax.broadcasted_iota(jnp.int32, (total, LANES), 1)
-    of_axis = []
-    for axis in (ROW, COL):
-        chosen = index == place + lax.axis_index(axis) * SIDE
-        of_axis.append(jnp.dot(known, chosen.astype(F32), preferred_element_type=F32))
-    row_mask, col_mask = of_axis
-    index = lax.broadcasted_iota(jnp.int32, (LANES, PIECE), 0)
-    place = lax.broadcasted_iota(jnp.int32, (LANES, PIECE), 1)
+    index = lax.broadcasted_iota(jnp.int32, (SIDE, PIECE), 0)
+    place = lax.broadcasted_iota(jnp.int32, (SIDE, PIECE), 1)
     for h in range(2):
         halves[h].wait()
         for at in range(h * HALF, (h + 1) * HALF, 8):
@@ -152,7 +157,8 @@
 def product(ref, wide, thin, left_ref, right_ref):
     core, half = lax.axis_index("core"), CH // 2
     start = pl.multiple_of((core if HALVES[0] == 0 else 1 - core) * half, half)
-    gather_k(ref[0, pl.ds(start, half), :].astype(F32), [TURN.index(z) for z in PAIRS], wide, thin, left_ref)
+    order = [TURN.index(z) for z in PAIRS]
+    gather_k(ref[0, pl.ds(start, half), :].astype(F32), order, wide, thin, left_ref)
     gather_k(ref[1].astype(F32), range(16), wide, thin, right_ref)
     return lax.dot_general(
         left_ref[...], right_ref[...], (((0,), (0,)), ((), ())), preferred_element_type=F32

time: 83.5 us -> 83 us (level)
  blocking collectives: 69.2 us -> 67.7 us
    all_to_all x1, blocking collectives: 43.1 us -> 42 us  [body(): lax.all_to_all(packed, ALL, 0, 0, axis_index_groups=groups(), tiled=True)]
where the time goes in v7:
time: 83 us; the launch traced here: 82.2 us
  blocking collectives  67.7 us (82%)
  Pallas kernels  10.2 us (12%)
  starting transfers between devices  3.38 us (4%)
  local copies, waits for them, and re-layouts  0.89 us (1%)
    all_to_all x1, blocking collectives, body(): lax.all_to_all(packed, ALL, 0, 0, axis_index_groups=groups(), tiled=True)  42 us
    all_to_all x1, blocking collectives, body(): lax.all_to_all(triangle, ALL, 0, 0, axis_index_groups=groups(), tiled=True)  25.7 us
    ppermute x1, starting transfers between devices, body(): got = lax.ppermute(mine, 'core', SWAP)  3.38 us
    pallas_call x1, Pallas kernels, body(): call(sides_kernel, (shape((2 * CH, BLOCK), BF16), shape((SIDE, SIDE, CH),...  3.2 us
    pallas_call x1, Pallas kernels, body(): call(beside_kernel, (shape((8 * SIDE, 16 * SIDE), F32), shape((BLOCK, CH)...  2.72 us
    pallas_call x1, Pallas kernels, body(): call(triangle_kernel, shape((2 * CH, SHARE), BF16), [*operands, vmem((6,...  2.51 us
    pallas_call x1, Pallas kernels, body(): call(finish_kernel, shape((SIDE, SIDE, CH), F32), [vmem((SIDE, SIDE, CH),...  1.8 us
  transfers between devices with their start and end apart: 1, of which 0 were waited for; matrix products, arithmetic and copies ran while one was open for 0% of the time, Pallas kernels for 3%

profile of v7, /device:TPU:1, one launch (start us, length us, event | category | flops | bytes accessed | tf_op | source)
XLA Modules:
  0.0 82.2 jit_solution(16670593445718827538)
XLA Ops:
  0.0 3.2 %shard_map.100 = (bf16[256,2304]{1,0:T(8,128)(2,1)S(1)}, bf16[48,48,128]{2,1,0:T(8,128)(2,1)S(1)}, bf16[128,128]{1,0:T(8,128)(2,1)S(1)}, f32[8,128]{1,0:T(8,128)S(1)}) custom-call(f32[48,48,128]{2,1,0:T(8,128)} %act_hbm.1, s32[768]{0:T(1024)} %mask_hbm.1, f32[128]{0:T(128)} %gain_hbm.2, f32[128]{0:T(128)} %bias_hbm.2, bf16[128,640]{1,0:T(8,128)(2,1)} %w_hbm.1, ...), custom_call_target="tpu_custom_call" | custom-call | flops 1000000000 | bytes 3000000 | tf_op jit(solution)/shard_map/pallas_call | solution.py:318
  3.2 0.5 reshape.6
  3.7 42.0 %all_to_all.10 = bf16[128,2,2304]{2,1,0:T(2,128)(2,1)S(1)} all-to-all(bf16[128,2,2304]{2,1,0:T(2,128)(2,1)S(1)} %reshape.6), channel_id=1, replica_groups={{109,45,173,141,13,205,237,77,103,39,167,135,7,199,231,71,99,35,163,131..., dimensions={0} | all-to-all | bytes 2359296 | tf_op jit(solution)/shard_map/all_to_all | solution.py:341
  45.7 0.1 copy.17
  45.8 3.4 %collective-permute-start = (bf16[2,128,2304]{2,1,0:T(8,128)(2,1)S(1)}, bf16[2,128,2304]{2,1,0:T(8,128)(2,1)S(1)}, u32[]{:S(2)}, u32[]{:S(2)}) collective-permute-start(bf16[2,128,2304]{2,1,0:T(8,128)(2,1)S(1)} %bitcast.6), channel_id=1, source_target_pairs={{0,16},{16,0},{1,17},{17,1},{2,18},{18,2},{3,19},{19,3},{4,20},{20... | collective-permute-start | bytes 3538952 | tf_op jit(solution)/shard_map/ppermute | solution.py:343
  49.2 2.7 %shard_map.101 = (f32[384,768]{1,0:T(8,128)S(1)}, f32[2304,128]{1,0:T(8,128)S(1)}, bf16[512,512]{1,0:T(8,128)(2,1)S(1)}, bf16[1024,1024]{1,0:T(8,128)(2,1)S(1)},...) custom-call(bf16[2,128,2304]{2,1,0:T(8,128)(2,1)S(1)} %bitcast.7, ...), custom_call_target="tpu_custom_call" | custom-call | flops 1000000000 | bytes 3000000 | tf_op jit(solution)/shard_map/pallas_call | solution.py:345
  51.9 0.0 collective-permute-done.got_ref
  51.9 2.5 %shard_map.102 = bf16[256,1152]{1,0:T(8,128)(2,1)S(1)} custom-call(f32[384,768]{1,0:T(8,128)S(1)} %get-tuple-element.21.part_ref, bf16[2,128,2304]{2,1,0:T(8,128)(2,1)S(1)} %collective-permute-done.got_ref, bf16[512,512]{1,0:T(8,128)(2,1)S(1)} %get-tuple-element.22.wide, bf16[1024,1024]{1,0:T(8,128)(2,1)S(1)} %get-tuple-element.23.thin), custom_call_target="tpu_custom_call" | custom-call | flops 1000000000 | bytes 3000000 | tf_op jit(solution)/shard_map/pallas_call | solution.py:360
  54.4 0.2 reshape.7
  54.7 25.7 %all_to_all.11 = bf16[128,2,1152]{2,1,0:T(2,128)(2,1)S(1)} all-to-all(bf16[128,2,1152]{2,1,0:T(2,128)(2,1)S(1)} %reshape.7), channel_id=1, replica_groups={{109,45,173,141,13,205,237,77,103,39,167,135,7,199,231,71,99,35,163,131..., dimensions={0} | all-to-all | bytes 1179648 | tf_op jit(solution)/shard_map/all_to_all | solution.py:366
  80.4 0.1 copy.18
  80.4 1.8 %shard_map.103 = f32[48,48,128]{2,1,0:T(8,128)} custom-call(bf16[2,128,1152]{2,1,0:T(8,128)(2,1)S(1)} %bitcast.8, f32[2304,128]{1,0:T(8,128)S(1)} %get-tuple-element.24.gate_ref, f32[128,128]{1,0:T(8,128)S(1)} %get-tuple-element.25.gain_ref, f32[128,128]{1,0:T(8,128)S(1)} %get-tuple-element.26.bias_ref, bf16[256,128]{1,0:T(8,128)(2,1)S(1)} %get-tuple-element.27.twice_ref, ...), custom_call_target="tpu_custom_call" | custom-call | flops 1000000000 | bytes 3000000 | tf_op jit(solution)/shard_map/pallas_call | solution.py:369
Async XLA Ops:
  45.8 6.1 %collective-permute-start = (bf16[2,128,2304]{2,1,0:T(8,128)(2,1)S(1)}, bf16[2,128,2304]{2,1,0:T(8,128)(2,1)S(1)}, u32[]{:S(2)}, u32[]{:S(2)}) collective-permute-start(bf16[2,128,2304]{2,1,0:T(8,128)(2,1)S(1)} %bitcast.6), channel_id=1, source_target_pairs={{0,16},{16,0},{1,17},{17,1},{2,18},{18,2},{3,19},{19,3},{4,20},{20... | collective-permute-start | bytes 3538952 | tf_op jit(solution)/shard_map/ppermute | solution.py:343

commit v8 on v7

--- a/solution.py
+++ b/solution.py
@@ -168,12 +168,14 @@
 def build_permutations(wide_ref, thin_ref):
     for ref, width in ((wide_ref, WIDE), (thin_ref, THIN)):
         count = LANES // width
-        size = count * LANES
-        lane = lax.broadcasted_iota(jnp.int32, (LANES, size), 1)
-        row = lax.broadcasted_iota(jnp.int32, (LANES, 1), 0)
+        ref[...] = jnp.zeros(ref.shape, BF16)
+        lane = lax.broadcasted_iota(jnp.int32, (width, LANES), 1)
+        row = lax.broadcasted_iota(jnp.int32, (width, LANES), 0)
         for g in range(count):
-            goes = (row // width * count + g) * width + row % width
-            ref[g * LANES : (g + 1) * LANES] = (lane == goes).astype(F32).astype(BF16)
+            one = (lane == g * width + row).astype(F32).astype(BF16)
+            for b in range(count):
+                at = g * LANES + b * width
+                ref[at : at + width, b * LANES : (b + 1) * LANES] = one
 
 
 def beside_kernel(

time: 83 us -> 82.9 us (level)
  no operation moved by 1% of the time
where the time goes in v8:
time: 82.9 us; the launch traced here: 81.9 us
  blocking collectives  67.4 us (81%)
  Pallas kernels  10.1 us (12%)
  starting transfers between devices  3.38 us (4%)
  local copies, waits for them, and re-layouts  0.89 us (1%)
    all_to_all x1, blocking collectives, body(): lax.all_to_all(packed, ALL, 0, 0, axis_index_groups=groups(), tiled=True)  42 us
    all_to_all x1, blocking collectives, body(): lax.all_to_all(triangle, ALL, 0, 0, axis_index_groups=groups(), tiled=True)  25.5 us
    ppermute x1, starting transfers between devices, body(): got = lax.ppermute(mine, 'core', SWAP)  3.38 us
    pallas_call x1, Pallas kernels, body(): call(sides_kernel, (shape((2 * CH, BLOCK), BF16), shape((SIDE, SIDE, CH),...  3.2 us
    pallas_call x1, Pallas kernels, body(): call(beside_kernel, (shape((8 * SIDE, 16 * SIDE), F32), shape((BLOCK, CH)...  2.62 us
    pallas_call x1, Pallas kernels, body(): call(triangle_kernel, shape((2 * CH, SHARE), BF16), [*operands, vmem((6,...  2.52 us
    pallas_call x1, Pallas kernels, body(): call(finish_kernel, shape((SIDE, SIDE, CH), F32), [vmem((SIDE, SIDE, CH),...  1.8 us
  transfers between devices with their start and end apart: 1, of which 0 were waited for; matrix products, arithmetic and copies ran while one was open for 0% of the time, Pallas kernels for 3%

profile of v8, /device:TPU:1, one launch (start us, length us, event | category | flops | bytes accessed | tf_op | source)
XLA Modules:
  0.0 81.9 jit_solution(663399062371701373)
XLA Ops:
  0.0 3.2 %shard_map.100 = (bf16[256,2304]{1,0:T(8,128)(2,1)S(1)}, bf16[48,48,128]{2,1,0:T(8,128)(2,1)S(1)}, bf16[128,128]{1,0:T(8,128)(2,1)S(1)}, f32[8,128]{1,0:T(8,128)S(1)}) custom-call(f32[48,48,128]{2,1,0:T(8,128)} %act_hbm.1, s32[768]{0:T(1024)} %mask_hbm.1, f32[128]{0:T(128)} %gain_hbm.2, f32[128]{0:T(128)} %bias_hbm.2, bf16[128,640]{1,0:T(8,128)(2,1)} %w_hbm.1, ...), custom_call_target="tpu_custom_call" | custom-call | flops 1000000000 | bytes 3000000 | tf_op jit(solution)/shard_map/pallas_call | solution.py:320
  3.2 0.5 reshape.6
  3.7 42.0 %all_to_all.10 = bf16[128,2,2304]{2,1,0:T(2,128)(2,1)S(1)} all-to-all(bf16[128,2,2304]{2,1,0:T(2,128)(2,1)S(1)} %reshape.6), channel_id=1, replica_groups={{109,45,173,141,13,205,237,77,103,39,167,135,7,199,231,71,99,35,163,131..., dimensions={0} | all-to-all | bytes 2359296 | tf_op jit(solution)/shard_map/all_to_all | solution.py:343
  45.7 0.1 copy.17
  45.8 3.4 %collective-permute-start = (bf16[2,128,2304]{2,1,0:T(8,128)(2,1)S(1)}, bf16[2,128,2304]{2,1,0:T(8,128)(2,1)S(1)}, u32[]{:S(2)}, u32[]{:S(2)}) collective-permute-start(bf16[2,128,2304]{2,1,0:T(8,128)(2,1)S(1)} %bitcast.6), channel_id=1, source_target_pairs={{0,16},{16,0},{1,17},{17,1},{2,18},{18,2},{3,19},{19,3},{4,20},{20... | collective-permute-start | bytes 3538952 | tf_op jit(solution)/shard_map/ppermute | solution.py:345
  49.2 2.6 %shard_map.101 = (f32[384,768]{1,0:T(8,128)S(1)}, f32[2304,128]{1,0:T(8,128)S(1)}, bf16[512,512]{1,0:T(8,128)(2,1)S(1)}, bf16[1024,1024]{1,0:T(8,128)(2,1)S(1)},...) custom-call(bf16[2,128,2304]{2,1,0:T(8,128)(2,1)S(1)} %bitcast.7, ...), custom_call_target="tpu_custom_call" | custom-call | flops 1000000000 | bytes 3000000 | tf_op jit(solution)/shard_map/pallas_call | solution.py:347
  51.8 0.0 collective-permute-done.got_ref
  51.8 2.5 %shard_map.102 = bf16[256,1152]{1,0:T(8,128)(2,1)S(1)} custom-call(f32[384,768]{1,0:T(8,128)S(1)} %get-tuple-element.21.part_ref, bf16[2,128,2304]{2,1,0:T(8,128)(2,1)S(1)} %collective-permute-done.got_ref, bf16[512,512]{1,0:T(8,128)(2,1)S(1)} %get-tuple-element.22.wide, bf16[1024,1024]{1,0:T(8,128)(2,1)S(1)} %get-tuple-element.23.thin), custom_call_target="tpu_custom_call" | custom-call | flops 1000000000 | bytes 3000000 | tf_op jit(solution)/shard_map/pallas_call | solution.py:362
  54.3 0.2 reshape.7
  54.6 25.5 %all_to_all.11 = bf16[128,2,1152]{2,1,0:T(2,128)(2,1)S(1)} all-to-all(bf16[128,2,1152]{2,1,0:T(2,128)(2,1)S(1)} %reshape.7), channel_id=1, replica_groups={{109,45,173,141,13,205,237,77,103,39,167,135,7,199,231,71,99,35,163,131..., dimensions={0} | all-to-all | bytes 1179648 | tf_op jit(solution)/shard_map/all_to_all | solution.py:368
  80.0 0.1 copy.18
  80.1 1.8 %shard_map.103 = f32[48,48,128]{2,1,0:T(8,128)} custom-call(bf16[2,128,1152]{2,1,0:T(8,128)(2,1)S(1)} %bitcast.8, f32[2304,128]{1,0:T(8,128)S(1)} %get-tuple-element.24.gate_ref, f32[128,128]{1,0:T(8,128)S(1)} %get-tuple-element.25.gain_ref, f32[128,128]{1,0:T(8,128)S(1)} %get-tuple-element.26.bias_ref, bf16[256,128]{1,0:T(8,128)(2,1)S(1)} %get-tuple-element.27.twice_ref, ...), custom_call_target="tpu_custom_call" | custom-call | flops 1000000000 | bytes 3000000 | tf_op jit(solution)/shard_map/pallas_call | solution.py:371
Async XLA Ops:
  45.8 6.0 %collective-permute-start = (bf16[2,128,2304]{2,1,0:T(8,128)(2,1)S(1)}, bf16[2,128,2304]{2,1,0:T(8,128)(2,1)S(1)}, u32[]{:S(2)}, u32[]{:S(2)}) collective-permute-start(bf16[2,128,2304]{2,1,0:T(8,128)(2,1)S(1)} %bitcast.6), channel_id=1, source_target_pairs={{0,16},{16,0},{1,17},{17,1},{2,18},{18,2},{3,19},{19,3},{4,20},{20... | collective-permute-start | bytes 3538952 | tf_op jit(solution)/shard_map/ppermute | solution.py:345

commit v9 on v8

--- a/solution.py
+++ b/solution.py
@@ -16,7 +16,8 @@
 SWAP = [(0, 1), (1, 0)]
 LANES = 128
 SIDE = 48
-HALF = SIDE // 2
+PARTS = 1
+PART = SIDE // PARTS
 WIDE = 32
 THIN = 16
 BLOCK = SIDE * SIDE
@@ -48,14 +49,14 @@
     out_ref, normed_ref, gate_w_ref, gate_b_ref,
     act, mask_v, gain_v, bias_v, w, wb, wt32, wt, wbt, sem,
 ):
-    halves = [
+    parts_in = [
         pltpu.make_async_copy(
-            act_hbm.at[h * HALF : (h + 1) * HALF], act.at[h * HALF : (h + 1) * HALF], sem.at[h]
-        )
-        for h in range(2)
+            act_hbm.at[h * PART : (h + 1) * PART], act.at[h * PART : (h + 1) * PART], sem.at[h]
+        )
+        for h in range(PARTS)
     ]
     small = [
-        pltpu.make_async_copy(src, dst, sem.at[2 + n])
+        pltpu.make_async_copy(src, dst, sem.at[PARTS + n])
         for n, (src, dst) in enumerate(
             (
                 (mask_hbm, mask_v.at[0]),
@@ -66,7 +67,7 @@
             )
         )
     ]
-    for copy in halves[:1] + small + halves[1:]:
+    for copy in parts_in[:1] + small + parts_in[1:]:
         copy.start()
     total = mask_v.shape[1]
     index = lax.broadcasted_iota(jnp.int32, (total, LANES), 0)
@@ -89,9 +90,9 @@
     gate_b_ref[...] = jnp.broadcast_to(wb[:, 4 * CH :], gate_b_ref.shape)
     index = lax.broadcasted_iota(jnp.int32, (SIDE, PIECE), 0)
     place = lax.broadcasted_iota(jnp.int32, (SIDE, PIECE), 1)
-    for h in range(2):
-        halves[h].wait()
-        for at in range(h * HALF, (h + 1) * HALF, 8):
+    for h in range(PARTS):
+        parts_in[h].wait()
+        for at in range(h * PART, (h + 1) * PART, 8):
             values = act[at : at + 8].reshape(8 * SIDE, LANES)
             off = values - jnp.mean(values, axis=-1, keepdims=True)
             spread = jnp.mean(jnp.square(off), axis=-1, keepdims=True)
@@ -335,7 +336,7 @@
             vmem((4 * CH, CH), F32),
             vmem((4 * CH, CH), BF16),
             vmem((4 * CH, LANES), F32),
-            pltpu.SemaphoreType.DMA((7,)),
+            pltpu.SemaphoreType.DMA((PARTS + 5,)),
         ],
         in_specs=[hbm] * 6,
     )(*stay((pair_act, residue_mask, norm_in_gain, norm_in_bias, proj_in, proj_bias)))

time: 82.9 us -> 82.7 us (level)
  no operation moved by 1% of the time
where the time goes in v9:
time: 82.7 us; the launch traced here: 81.8 us
  blocking collectives  67.5 us (82%)
  Pallas kernels  9.98 us (12%)
  starting transfers between devices  3.37 us (4%)
  local copies, waits for them, and re-layouts  0.89 us (1%)
    all_to_all x1, blocking collectives, body(): lax.all_to_all(packed, ALL, 0, 0, axis_index_groups=groups(), tiled=True)  42 us
    all_to_all x1, blocking collectives, body(): lax.all_to_all(triangle, ALL, 0, 0, axis_index_groups=groups(), tiled=True)  25.5 us
    ppermute x1, starting transfers between devices, body(): got = lax.ppermute(mine, 'core', SWAP)  3.37 us
    pallas_call x1, Pallas kernels, body(): call(sides_kernel, (shape((2 * CH, BLOCK), BF16), shape((SIDE, SIDE, CH),...  3.05 us
    pallas_call x1, Pallas kernels, body(): call(beside_kernel, (shape((8 * SIDE, 16 * SIDE), F32), shape((BLOCK, CH)...  2.61 us
    pallas_call x1, Pallas kernels, body(): call(triangle_kernel, shape((2 * CH, SHARE), BF16), [*operands, vmem((6,...  2.52 us
    pallas_call x1, Pallas kernels, body(): call(finish_kernel, shape((SIDE, SIDE, CH), F32), [vmem((SIDE, SIDE, CH),...  1.8 us
  transfers between devices with their start and end apart: 1, of which 0 were waited for; matrix products, arithmetic and copies ran while one was open for 0% of the time, Pallas kernels for 3%

profile of v9, /device:TPU:1, one launch (start us, length us, event | category | flops | bytes accessed | tf_op | source)
XLA Modules:
  0.0 81.8 jit_solution(14285328128029235532)
XLA Ops:
  0.0 3.0 %shard_map.100 = (bf16[256,2304]{1,0:T(8,128)(2,1)S(1)}, bf16[48,48,128]{2,1,0:T(8,128)(2,1)S(1)}, bf16[128,128]{1,0:T(8,128)(2,1)S(1)}, f32[8,128]{1,0:T(8,128)S(1)}) custom-call(f32[48,48,128]{2,1,0:T(8,128)} %act_hbm.1, s32[768]{0:T(1024)} %mask_hbm.1, f32[128]{0:T(128)} %gain_hbm.2, f32[128]{0:T(128)} %bias_hbm.2, bf16[128,640]{1,0:T(8,128)(2,1)} %w_hbm.1, ...), custom_call_target="tpu_custom_call" | custom-call | flops 1000000000 | bytes 3000000 | tf_op jit(solution)/shard_map/pallas_call | solution.py:321
  3.1 0.5 reshape.6
  3.6 42.0 %all_to_all.10 = bf16[128,2,2304]{2,1,0:T(2,128)(2,1)S(1)} all-to-all(bf16[128,2,2304]{2,1,0:T(2,128)(2,1)S(1)} %reshape.6), channel_id=1, replica_groups={{109,45,173,141,13,205,237,77,103,39,167,135,7,199,231,71,99,35,163,131..., dimensions={0} | all-to-all | bytes 2359296 | tf_op jit(solution)/shard_map/all_to_all | solution.py:344
  45.5 0.1 copy.17
  45.7 3.4 %collective-permute-start = (bf16[2,128,2304]{2,1,0:T(8,128)(2,1)S(1)}, bf16[2,128,2304]{2,1,0:T(8,128)(2,1)S(1)}, u32[]{:S(2)}, u32[]{:S(2)}) collective-permute-start(bf16[2,128,2304]{2,1,0:T(8,128)(2,1)S(1)} %bitcast.6), channel_id=1, source_target_pairs={{0,16},{16,0},{1,17},{17,1},{2,18},{18,2},{3,19},{19,3},{4,20},{20... | collective-permute-start | bytes 3538952 | tf_op jit(solution)/shard_map/ppermute | solution.py:346
  49.0 2.6 %shard_map.101 = (f32[384,768]{1,0:T(8,128)S(1)}, f32[2304,128]{1,0:T(8,128)S(1)}, bf16[512,512]{1,0:T(8,128)(2,1)S(1)}, bf16[1024,1024]{1,0:T(8,128)(2,1)S(1)},...) custom-call(bf16[2,128,2304]{2,1,0:T(8,128)(2,1)S(1)} %bitcast.7, ...), custom_call_target="tpu_custom_call" | custom-call | flops 1000000000 | bytes 3000000 | tf_op jit(solution)/shard_map/pallas_call | solution.py:348
  51.6 0.0 collective-permute-done.got_ref
  51.7 2.5 %shard_map.102 = bf16[256,1152]{1,0:T(8,128)(2,1)S(1)} custom-call(f32[384,768]{1,0:T(8,128)S(1)} %get-tuple-element.21.part_ref, bf16[2,128,2304]{2,1,0:T(8,128)(2,1)S(1)} %collective-permute-done.got_ref, bf16[512,512]{1,0:T(8,128)(2,1)S(1)} %get-tuple-element.22.wide, bf16[1024,1024]{1,0:T(8,128)(2,1)S(1)} %get-tuple-element.23.thin), custom_call_target="tpu_custom_call" | custom-call | flops 1000000000 | bytes 3000000 | tf_op jit(solution)/shard_map/pallas_call | solution.py:363
  54.2 0.2 reshape.7
  54.4 25.5 %all_to_all.11 = bf16[128,2,1152]{2,1,0:T(2,128)(2,1)S(1)} all-to-all(bf16[128,2,1152]{2,1,0:T(2,128)(2,1)S(1)} %reshape.7), channel_id=1, replica_groups={{109,45,173,141,13,205,237,77,103,39,167,135,7,199,231,71,99,35,163,131..., dimensions={0} | all-to-all | bytes 1179648 | tf_op jit(solution)/shard_map/all_to_all | solution.py:369
  79.9 0.1 copy.18
  80.0 1.8 %shard_map.103 = f32[48,48,128]{2,1,0:T(8,128)} custom-call(bf16[2,128,1152]{2,1,0:T(8,128)(2,1)S(1)} %bitcast.8, f32[2304,128]{1,0:T(8,128)S(1)} %get-tuple-element.24.gate_ref, f32[128,128]{1,0:T(8,128)S(1)} %get-tuple-element.25.gain_ref, f32[128,128]{1,0:T(8,128)S(1)} %get-tuple-element.26.bias_ref, bf16[256,128]{1,0:T(8,128)(2,1)S(1)} %get-tuple-element.27.twice_ref, ...), custom_call_target="tpu_custom_call" | custom-call | flops 1000000000 | bytes 3000000 | tf_op jit(solution)/shard_map/pallas_call | solution.py:372
Async XLA Ops:
  45.7 6.0 %collective-permute-start = (bf16[2,128,2304]{2,1,0:T(8,128)(2,1)S(1)}, bf16[2,128,2304]{2,1,0:T(8,128)(2,1)S(1)}, u32[]{:S(2)}, u32[]{:S(2)}) collective-permute-start(bf16[2,128,2304]{2,1,0:T(8,128)(2,1)S(1)} %bitcast.6), channel_id=1, source_target_pairs={{0,16},{16,0},{1,17},{17,1},{2,18},{18,2},{3,19},{19,3},{4,20},{20... | collective-permute-start | bytes 3538952 | tf_op jit(solution)/shard_map/ppermute | solution.py:346

commit v10 on v9

--- a/solution.py
+++ b/solution.py
@@ -10,8 +10,8 @@
 ROW = ("y_lo", "x", "core")
 COL = ("z", "y_hi")
 ALL = ROW + COL
-TURN = (6, 3, 1, 0, 7, 2, 5, 4)
-PAIRS = (3, 1, 5, 4, 0, 6, 7, 2)
+TURN = (4, 7, 1, 2, 6, 0, 5, 3)
+PAIRS = (2, 6, 1, 0, 7, 5, 3, 4)
 HALVES = (1, 0)
 SWAP = [(0, 1), (1, 0)]
 LANES = 128

time: 82.7 us -> 82.9 us (level)
  blocking collectives: 67.5 us -> 70.3 us
  starting transfers between devices: 3.37 us -> 1.44 us
    ppermute x1, starting transfers between devices: 3.37 us -> 1.44 us  [body(): got = lax.ppermute(mine, 'core', SWAP)]
    all_to_all x1, blocking collectives: 42 us -> 43.6 us  [body(): lax.all_to_all(packed, ALL, 0, 0, axis_index_groups=groups(), tiled=True)]
    all_to_all x1, blocking collectives: 25.5 us -> 26.7 us  [body(): lax.all_to_all(triangle, ALL, 0, 0, axis_index_groups=groups(), tiled=True)]
where the time goes in v10:
time: 82.9 us; the launch traced here: 82.7 us
  blocking collectives  70.3 us (85%)
  Pallas kernels  9.97 us (12%)
  starting transfers between devices  1.44 us (2%)
  local copies, waits for them, and re-layouts  0.89 us (1%)
    all_to_all x1, blocking collectives, body(): lax.all_to_all(packed, ALL, 0, 0, axis_index_groups=groups(), tiled=True)  43.6 us
    all_to_all x1, blocking collectives, body(): lax.all_to_all(triangle, ALL, 0, 0, axis_index_groups=groups(), tiled=True)  26.7 us
    pallas_call x1, Pallas kernels, body(): call(sides_kernel, (shape((2 * CH, BLOCK), BF16), shape((SIDE, SIDE, CH),...  3.05 us
    pallas_call x1, Pallas kernels, body(): call(beside_kernel, (shape((8 * SIDE, 16 * SIDE), F32), shape((BLOCK, CH)...  2.61 us
    pallas_call x1, Pallas kernels, body(): call(triangle_kernel, shape((2 * CH, SHARE), BF16), [*operands, vmem((6,...  2.51 us
    pallas_call x1, Pallas kernels, body(): call(finish_kernel, shape((SIDE, SIDE, CH), F32), [vmem((SIDE, SIDE, CH),...  1.8 us
  transfers between devices with their start and end apart: 1, of which 0 were waited for; matrix products, arithmetic and copies ran while one was open for 0% of the time, Pallas kernels for 3%

profile of v10, /device:TPU:1, one launch (start us, length us, event | category | flops | bytes accessed | tf_op | source)
XLA Modules:
  0.0 82.7 jit_solution(5461093579839995816)
XLA Ops:
  0.0 3.0 %shard_map.100 = (bf16[256,2304]{1,0:T(8,128)(2,1)S(1)}, bf16[48,48,128]{2,1,0:T(8,128)(2,1)S(1)}, bf16[128,128]{1,0:T(8,128)(2,1)S(1)}, f32[8,128]{1,0:T(8,128)S(1)}) custom-call(f32[48,48,128]{2,1,0:T(8,128)} %act_hbm.1, s32[768]{0:T(1024)} %mask_hbm.1, f32[128]{0:T(128)} %gain_hbm.2, f32[128]{0:T(128)} %bias_hbm.2, bf16[128,640]{1,0:T(8,128)(2,1)} %w_hbm.1, ...), custom_call_target="tpu_custom_call" | custom-call | flops 1000000000 | bytes 3000000 | tf_op jit(solution)/shard_map/pallas_call | solution.py:321
  3.1 0.5 reshape.6
  3.6 43.6 %all_to_all.10 = bf16[128,2,2304]{2,1,0:T(2,128)(2,1)S(1)} all-to-all(bf16[128,2,2304]{2,1,0:T(2,128)(2,1)S(1)} %reshape.6), channel_id=1, replica_groups={{73,201,41,9,233,169,105,137,79,207,47,15,239,175,111,143,67,195,35,3,2..., dimensions={0} | all-to-all | bytes 2359296 | tf_op jit(solution)/shard_map/all_to_all | solution.py:344
  47.1 0.1 copy.17
  47.2 1.4 %collective-permute-start = (bf16[2,128,2304]{2,1,0:T(8,128)(2,1)S(1)}, bf16[2,128,2304]{2,1,0:T(8,128)(2,1)S(1)}, u32[]{:S(2)}, u32[]{:S(2)}) collective-permute-start(bf16[2,128,2304]{2,1,0:T(8,128)(2,1)S(1)} %bitcast.6), channel_id=1, source_target_pairs={{0,16},{16,0},{1,17},{17,1},{2,18},{18,2},{3,19},{19,3},{4,20},{20... | collective-permute-start | bytes 3538952 | tf_op jit(solution)/shard_map/ppermute | solution.py:346
  48.7 2.6 %shard_map.101 = (f32[384,768]{1,0:T(8,128)S(1)}, f32[2304,128]{1,0:T(8,128)S(1)}, bf16[512,512]{1,0:T(8,128)(2,1)S(1)}, bf16[1024,1024]{1,0:T(8,128)(2,1)S(1)},...) custom-call(bf16[2,128,2304]{2,1,0:T(8,128)(2,1)S(1)} %bitcast.7, ...), custom_call_target="tpu_custom_call" | custom-call | flops 1000000000 | bytes 3000000 | tf_op jit(solution)/shard_map/pallas_call | solution.py:348
  51.3 0.0 collective-permute-done.got_ref
  51.3 2.5 %shard_map.102 = bf16[256,1152]{1,0:T(8,128)(2,1)S(1)} custom-call(f32[384,768]{1,0:T(8,128)S(1)} %get-tuple-element.21.part_ref, bf16[2,128,2304]{2,1,0:T(8,128)(2,1)S(1)} %collective-permute-done.got_ref, bf16[512,512]{1,0:T(8,128)(2,1)S(1)} %get-tuple-element.22.wide, bf16[1024,1024]{1,0:T(8,128)(2,1)S(1)} %get-tuple-element.23.thin), custom_call_target="tpu_custom_call" | custom-call | flops 1000000000 | bytes 3000000 | tf_op jit(solution)/shard_map/pallas_call | solution.py:363
  53.8 0.2 reshape.7
  54.1 26.7 %all_to_all.11 = bf16[128,2,1152]{2,1,0:T(2,128)(2,1)S(1)} all-to-all(bf16[128,2,1152]{2,1,0:T(2,128)(2,1)S(1)} %reshape.7), channel_id=1, replica_groups={{73,201,41,9,233,169,105,137,79,207,47,15,239,175,111,143,67,195,35,3,2..., dimensions={0} | all-to-all | bytes 1179648 | tf_op jit(solution)/shard_map/all_to_all | solution.py:369
  80.8 0.1 copy.18
  80.9 1.8 %shard_map.103 = f32[48,48,128]{2,1,0:T(8,128)} custom-call(bf16[2,128,1152]{2,1,0:T(8,128)(2,1)S(1)} %bitcast.8, f32[2304,128]{1,0:T(8,128)S(1)} %get-tuple-element.24.gate_ref, f32[128,128]{1,0:T(8,128)S(1)} %get-tuple-element.25.gain_ref, f32[128,128]{1,0:T(8,128)S(1)} %get-tuple-element.26.bias_ref, bf16[256,128]{1,0:T(8,128)(2,1)S(1)} %get-tuple-element.27.twice_ref, ...), custom_call_target="tpu_custom_call" | custom-call | flops 1000000000 | bytes 3000000 | tf_op jit(solution)/shard_map/pallas_call | solution.py:372
Async XLA Ops:
  47.2 4.1 %collective-permute-start = (bf16[2,128,2304]{2,1,0:T(8,128)(2,1)S(1)}, bf16[2,128,2304]{2,1,0:T(8,128)(2,1)S(1)}, u32[]{:S(2)}, u32[]{:S(2)}) collective-permute-start(bf16[2,128,2304]{2,1,0:T(8,128)(2,1)S(1)} %bitcast.6), channel_id=1, source_target_pairs={{0,16},{16,0},{1,17},{17,1},{2,18},{18,2},{3,19},{19,3},{4,20},{20... | collective-permute-start | bytes 3538952 | tf_op jit(solution)/shard_map/ppermute | solution.py:346
